TPU v7x, 32 devices: a whole 2x2x4 slice. The times are simulated.
32 devices in a mesh: groups: 2 (over y), expert: 8 (over z, x), replica: 2 (over core).
Axes of the slice: x: 2, y: 2, z: 4, core: 2. Of those that a mesh axis runs over, the one named last changes fastest.
Arguments:
- encoded: bfloat16 [32768, 128], P(('groups', 'expert', 'replica')), parts along dimension 0, may hold values from -6 to 6
- region_id: int32 [32768], P(('groups', 'expert', 'replica')), parts along dimension 0, may hold values from 0 to 15, as said below
- spacing: float32 [32768], P(('groups', 'expert', 'replica')), parts along dimension 0, may hold values from 0.01 to 0.1
- frame_index: int32 [512], P(('groups', 'expert', 'replica')), parts along dimension 0, may hold values from 0 to 255
- target_rgb: float32 [3, 512], P(None, ('groups', 'expert', 'replica')), parts along dimension 1, may hold values from 0 to 1
- frame_code: float32 [3, 512], P(None, 'groups'), parts along dimension 1, may hold values from -4 to 4
- first_weight: bfloat16 [16, 128, 256], P('expert'), may hold values from -0.5 to 0.5
- hidden_weight: bfloat16 [16, 3, 256, 256], P('expert'), may hold values from -0.375 to 0.375
- head_weight: bfloat16 [4, 256], replicated, may hold values from -0.375 to 0.375
Outputs:
- first_grad: float32 [32, 128, 256], P(('groups', 'expert'), 'replica'), parts along dimension 0
- hidden_grad: float32 [32, 3, 256, 256], P(('groups', 'expert'), None, 'replica'), parts along dimension 0
- head_grad: float32 [8, 256], P('groups'), parts along dimension 0
- rendered: float32 [3, 512], P(None, ('groups', 'expert', 'replica')), parts along dimension 1
There are 2 independent parts, one for each index of `groups`. A program takes and returns all parts, laid end to end along the dimension named above; an argument that names none is the same for every part. Nothing has to cross between parts.
Inputs may be any that keep to these rules, and one draw needn't show every extreme that they name: `region_id`: among the samples of one device no region is named more than 128 times, and some region is named exactly 128 times.
All inputs are finite; a program needn't handle non-finite values.
Results may differ from a plain program's by a relative error of at most 0.012.
Values may be sent and summed in bfloat16 or wider, within the bound.
No kernel may reach another device: no remote copies, remote signals or barrier semaphores. Data moves between devices by JAX's collectives and lax.ppermute only.
A program may use at most 64 MiB of HBM per device.

v0:
```python
import jax
import jax.numpy as jnp
from jax import lax
from jax.sharding import PartitionSpec as P

RAY_SAMPLES = 64


def silu_slope(linear):
    sigmoid_val = jax.nn.sigmoid(linear)
    return sigmoid_val * (1.0 + linear * (1.0 - sigmoid_val))


def composite(raw_in, spacing, frame_bias, target_rgb):
    ray_count = spacing.shape[0] // RAY_SAMPLES
    density = jax.nn.softplus(raw_in[0]).reshape(ray_count, RAY_SAMPLES)
    optical = density * spacing.reshape(ray_count, RAY_SAMPLES)
    before = jnp.cumsum(optical, axis=1) - optical
    weight = jnp.exp(-before) * (1.0 - jnp.exp(-optical))
    colour = jax.nn.sigmoid(raw_in[1:].reshape(3, ray_count, RAY_SAMPLES) + frame_bias[:, :, None])
    rendered = jnp.sum(weight[None] * colour, axis=2) + (1.0 - jnp.sum(weight, axis=1))[None]
    loss_value = 0.5 * jnp.sum((rendered - target_rgb) ** 2)
    return (loss_value, rendered)


def per_device(
    encoded,
    region_id,
    spacing,
    frame_index,
    target_rgb,
    frame_code,
    first_weight,
    hidden_weight,
    head_weight,
):
    owners = lax.axis_size("expert")
    local_count = first_weight.shape[0]
    experts = owners * local_count
    samples = encoded.shape[0]
    capacity = 2 * samples // experts
    enc_width = encoded.shape[1]
    hid_width = first_weight.shape[2]
    layer_count = hidden_weight.shape[1] + 1
    onehot = (region_id[:, None] == jnp.arange(experts, dtype=jnp.int32)[None, :]).astype(jnp.int32)
    running = jnp.cumsum(onehot, axis=0)
    slot_index = region_id * capacity + jnp.sum(running * onehot, axis=1) - 1
    outbound = jnp.zeros((experts * capacity, enc_width), jnp.bfloat16).at[slot_index].set(encoded)
    outbound = outbound.reshape(owners, local_count, capacity, enc_width)
    head_w32 = head_weight.astype(jnp.float32)
    row_block = lax.all_to_all(outbound, "expert", split_axis=0, concat_axis=0, tiled=True)
    activations = [row_block]
    slopes = []
    current = row_block
    for forward_layer_index in range(layer_count):
        forward_weight = (
            first_weight if forward_layer_index == 0 else hidden_weight[:, forward_layer_index - 1]
        )
        linear = jnp.einsum(
            "sxmi,xih->sxmh", current, forward_weight, preferred_element_type=jnp.float32
        )
        slopes.append(lax.optimization_barrier(silu_slope(linear).astype(jnp.bfloat16)))
        current = lax.optimization_barrier(jax.nn.silu(linear).astype(jnp.bfloat16))
        activations.append(current)
    produced = current
    produced, activations, slopes = (produced, tuple(activations), tuple(slopes))
    frame_hot = (
        frame_index[None, :] == jnp.arange(frame_code.shape[1], dtype=jnp.int32)[:, None]
    ).astype(jnp.float32)
    frame_bias = jnp.dot(frame_code, frame_hot, precision=lax.Precision.HIGHEST)
    returned = lax.all_to_all(produced, "expert", split_axis=0, concat_axis=0, tiled=True)
    feature_rows = returned.reshape(experts * capacity, hid_width)[slot_index]
    raw_t = jnp.einsum("ch,sh->cs", head_weight, feature_rows, preferred_element_type=jnp.float32)
    loss_value, pullback, rendered = jax.vjp(
        lambda raw_in: composite(raw_in, spacing, frame_bias, target_rgb), raw_t, has_aux=True
    )
    graw_t = pullback(jnp.ones((), jnp.float32))[0]
    head_part = jnp.dot(graw_t, feature_rows.astype(jnp.float32), precision=lax.Precision.HIGHEST)
    feature_pull = jnp.dot(graw_t.T, head_w32, precision=lax.Precision.HIGHEST).astype(jnp.bfloat16)
    grad_out = (
        jnp.zeros((experts * capacity, hid_width), jnp.bfloat16).at[slot_index].set(feature_pull)
    )
    grad_out = grad_out.reshape(owners, local_count, capacity, hid_width)
    upstream = lax.all_to_all(grad_out, "expert", split_axis=0, concat_axis=0, tiled=True)
    upstream = lax.optimization_barrier(upstream)
    grads = [None] * layer_count
    for layer_index in reversed(range(layer_count)):
        weight = first_weight if layer_index == 0 else hidden_weight[:, layer_index - 1]
        grad_linear = (
            upstream.astype(jnp.float32) * slopes[layer_index].astype(jnp.float32)
        ).astype(jnp.bfloat16)
        grads[layer_index] = jnp.einsum(
            "sxmi,sxmh->xih",
            activations[layer_index],
            grad_linear,
            preferred_element_type=jnp.float32,
        )
        if layer_index > 0:
            upstream = lax.optimization_barrier(
                jnp.einsum(
                    "sxmh,xih->sxmi", grad_linear, weight, preferred_element_type=jnp.float32
                ).astype(jnp.bfloat16)
            )
    first_grad, hidden_grad = (
        lax.psum_scatter(grads[0], "replica", scatter_dimension=1, tiled=True),
        lax.psum_scatter(jnp.stack(grads[1:], axis=1), "replica", scatter_dimension=2, tiled=True),
    )
    head_grad = lax.psum(head_part, ("expert", "replica"))
    return (first_grad, hidden_grad, head_grad, rendered)


def solution(mesh):
    placed = (
        P(("groups", "expert", "replica"), None),
        P(("groups", "expert", "replica")),
        P(("groups", "expert", "replica")),
        P(("groups", "expert", "replica")),
        P(None, ("groups", "expert", "replica")),
        P(None, "groups"),
        P("expert", None, None),
        P("expert", None, None, None),
        P(),
    )
    return jax.shard_map(
        per_device,
        mesh=mesh,
        in_specs=placed,
        out_specs=(
            P(("groups", "expert"), "replica", None),
            P(("groups", "expert"), None, "replica", None),
            P("groups", None),
            P(None, ("groups", "expert", "replica")),
        ),
        check_vma=False,
    )
```

profile of v0, /device:TPU:0, one launch (start us, length us, event | category | flops | bytes accessed | tf_op | source)
XLA Modules:
  0.0 171.8 jit_solution(12499045849482268776)
XLA Ops:
  7.2 0.7 fusion.57
  7.9 4.5 %reduce-window.6 = s32[16,8,128]{2,1,0:T(8,128)S(1)} reduce-window(s32[16,8,128]{2,1,0:T(8,128)S(1)} %fusion.57, s32[]{:T(128)} %constant.22.clone.1), window={size=1x1x128 pad=0_0x0_0x127_0}, to_apply=%region_0.0 | reduce-window | flops 2080768 | bytes 131076 | tf_op jit(solution)/shard_map/reduce-window
  12.4 0.1 slice.33
  12.5 0.1 copy.36
  12.7 0.1 broadcast_add_fusion
  12.8 0.7 fusion.55
  13.5 0.7 broadcast_clamp_fusion
  14.2 3.7 %scatter_custom_fusion = bf16[2048,128]{1,0:T(8,128)(2,1)S(1)} fusion(s32[1024]{0:T(1024)S(1)} %get-tuple-element.24, bf16[1024,128]{1,0:T(8,128)(2,1)} %param.9, bf16[]{:T(256)} %constant.18.clone.1), kind=kCustom, calls=%fused_computation.75 | custom fusion | bytes 524800 | tf_op jit(solution)/shard_map/scatter | solution.py:48
  17.9 21.6 %all_to_all.15 = bf16[8,2,128,128]{3,2,1,0:T(8,128)(2,1)S(1)} all-to-all(bf16[8,2,128,128]{3,2,1,0:T(8,128)(2,1)S(1)} %bitcast.191), channel_id=1, replica_groups=mesh['groups'=2,'expert'=8,'replica'=2] {'expert'}, dimensions={0} | all-to-all | bytes 1048576 | tf_op jit(solution)/shard_map/all_to_all | solution.py:51
  39.5 2.0 %fusion.24 = (bf16[8,2,128,256]{3,2,0,1:T(8,128)(2,1)S(1)}, bf16[8,2,128,256]{3,2,0,1:T(8,128)(2,1)}) fusion(bf16[2,128,256]{2,1,0:T(8,128)(2,1)S(1)} %copy-done, bf16[8,2,128,128]{3,2,1,0:T(8,128)(2,1)S(1)} %all_to_all.15), kind=kOutput, calls=%fused_computation.39 | convolution fusion | flops 139460608 | bytes 2752512 | tf_op jit(solution)/shard_map/sxmi,xih->sxmh/dot_general | solution.py:59
  41.6 1.1 fusion.17
  42.7 2.1 %fusion.10 = (bf16[8,2,128,256]{3,2,0,1:T(8,128)(2,1)S(1)}, bf16[8,2,128,256]{3,2,0,1:T(8,128)(2,1)}) fusion(bf16[8,2,128,256]{3,2,0,1:T(8,128)(2,1)S(1)} %get-tuple-element.29, bf16[2,3,256,256]{3,2,1,0:T(8,128)(2,1)S(1)} %copy-done.9), kind=kOutput, calls=%fused_computation.19 | convolution fusion | flops 273678336 | bytes 3407872 | tf_op jit(solution)/shard_map/sxmi,xih->sxmh/dot_general | solution.py:59
  44.8 2.1 %fusion.3 = (bf16[8,2,128,256]{3,2,0,1:T(8,128)(2,1)S(1)}, bf16[8,2,128,256]{3,2,0,1:T(8,128)(2,1)}) fusion(bf16[8,2,128,256]{3,2,0,1:T(8,128)(2,1)S(1)} %get-tuple-element.27, bf16[2,3,256,256]{3,2,1,0:T(8,128)(2,1)S(1)} %copy-done.9), kind=kOutput, calls=%fused_computation.9 | convolution fusion | flops 273678336 | bytes 3407872 | tf_op jit(solution)/shard_map/sxmi,xih->sxmh/dot_general | solution.py:59
  46.8 1.1 copy.42
  47.9 3.7 %all-to-all-start.1 = ((bf16[8,2,128,256]{3,2,1,0:T(8,128)(2,1)}), bf16[8,2,128,256]{3,2,1,0:T(8,128)(2,1)S(1)}, u32[]{:S(2)}, u32[]{:S(2)}) async-start(bf16[8,2,128,256]{3,2,1,0:T(8,128)(2,1)} %copy.42), calls=%async_computation.1 | async-start | bytes 2097152 | tf_op jit(solution)/shard_map/all_to_all | solution.py:71
  51.7 0.2 convolution_bitcast_fusion.5
  51.9 0.1 add.103
  52.0 0.1 add.108
  52.1 25.2 %all-to-all-done.1 = bf16[8,2,128,256]{3,2,1,0:T(8,128)(2,1)S(1)} async-done(((bf16[8,2,128,256]{3,2,1,0:T(8,128)(2,1)}), bf16[8,2,128,256]{3,2,1,0:T(8,128)(2,1)S(1)}, u32[]{:S(2)}, u32[]{:S(2)}) %all-to-all-start.1) | async-done | bytes 1048608 | tf_op jit(solution)/shard_map/all_to_all | solution.py:71
  77.3 3.9 %gather_fusion = bf16[1024,256]{1,0:T(8,128)(2,1)S(1)} fusion(bf16[2048,256]{1,0:T(8,128)(2,1)S(1)} %bitcast.189, s32[1024]{0:T(1024)S(1)} %get-tuple-element.23), kind=kCustom, calls=%fused_computation | custom fusion | bytes 1052672 | tf_op jit(solution)/shard_map/gather | solution.py:72
  81.2 0.2 convolution_bitcast_fusion.4
  81.6 0.2 reduce_window_sum.43
  81.9 0.1 fusion.69
  82.0 0.1 reshape.112
  82.1 0.2 multiply_reduce_fusion
  82.3 0.6 fusion.68
  83.1 0.1 broadcast_in_dim.37
  83.3 0.1 multiply_negate_fusion
  83.4 0.4 reduce_window_sum.45
  83.9 0.7 convolution_convert_fusion.3
  84.6 6.0 %scatter_custom_fusion.1 = bf16[2048,256]{1,0:T(8,128)(2,1)} fusion(s32[1024]{0:T(1024)S(1)} %get-tuple-element.24, bf16[1024,256]{1,0:T(8,128)(2,1)S(1)} %convolution_convert_fusion.3, bf16[]{:T(256)} %constant.18.clone.1), kind=kCustom, calls=%fused_computation.64 | custom fusion | bytes 1048578 | tf_op jit(solution)/shard_map/scatter | solution.py:81
  90.7 3.6 %all-to-all-start.2 = ((bf16[8,2,128,256]{3,2,1,0:T(8,128)(2,1)}), bf16[8,2,128,256]{3,2,1,0:T(8,128)(2,1)S(1)}, u32[]{:S(2)}, u32[]{:S(2)}) async-start(bf16[8,2,128,256]{3,2,1,0:T(8,128)(2,1)} %bitcast.190), calls=%async_computation.2 | async-start | bytes 2097152 | tf_op jit(solution)/shard_map/all_to_all | solution.py:84
  94.2 0.2 reduce-scatter.5.cloned.1.call-start
  94.4 25.6 %all-to-all-done.2 = bf16[8,2,128,256]{3,2,1,0:T(8,128)(2,1)S(1)} async-done(((bf16[8,2,128,256]{3,2,1,0:T(8,128)(2,1)}), bf16[8,2,128,256]{3,2,1,0:T(8,128)(2,1)S(1)}, u32[]{:S(2)}, u32[]{:S(2)}) %all-to-all-start.2) | async-done | bytes 1048608 | tf_op jit(solution)/shard_map/all_to_all | solution.py:84
  120.0 2.3 %convolution_bitcast_fusion = f32[2,1,256,256]{3,2,0,1:T(8,128)S(1)} fusion(bf16[8,2,128,256]{3,2,0,1:T(8,128)(2,1)} %copy-done.6, bf16[8,2,128,256]{3,2,0,1:T(8,128)(2,1)} %get-tuple-element.26, bf16[8,2,128,256]{3,2,1,0:T(8,128)(2,1)S(1)} %all-to-all-done.2), kind=kOutput, calls=%fused_computation.55 | convolution fusion | flops 270532608 | bytes 3670016 | tf_op jit(solution)/shard_map/sxmi,sxmh->xih/dot_general | solution.py:92
  122.3 0.5 fusion.28
  122.9 0.7 copy-done.1
  123.6 0.3 copy-done.5
  123.9 0.6 convolution_bitcast_fusion.1
  124.5 0.5 fusion.29
  125.0 0.7 copy-done.3
  125.7 0.6 convolution_bitcast_fusion.2
  126.4 1.3 pad_maximum_fusion
  127.7 1.5 fusion.30
  129.3 1.2 convolution_bitcast_fusion.3
  130.5 0.3 fusion.59
  130.8 32.1 %psum.7 = f32[4,256]{1,0:T(4,128)} all-reduce(f32[4,256]{1,0:T(4,128)S(1)} %fusion.59), channel_id=1, replica_groups=mesh['groups'=2,'expert'=8,'replica'=2] {'expert','replica'}, use_global_device_ids=true, to_apply=%region_13.14 | all-reduce | flops 1024 | bytes 8192 | tf_op jit(solution)/shard_map/psum | solution.py:108
  162.8 2.1 %copy.48 = f32[2,3,128,256]{3,2,1,0:T(8,128)} copy(f32[2,3,128,256]{3,2,0,1:T(8,128)} %reduce-scatter.5.cloned.1.call-done) | data formatting | bytes 1572864
  (54 shorter events, 1.0 us)
Async XLA Ops:
  7.2 32.3 %copy-start = (bf16[2,128,256]{2,1,0:T(8,128)(2,1)S(1)}, bf16[2,128,256]{2,1,0:T(8,128)(2,1)}, u32[]{:S(2)}) copy-start(bf16[2,128,256]{2,1,0:T(8,128)(2,1)} %param.15) | copy-start | bytes 393220
  39.5 2.1 %copy-start.9 = (bf16[2,3,256,256]{3,2,1,0:T(8,128)(2,1)S(1)}, bf16[2,3,256,256]{3,2,1,0:T(8,128)(2,1)}, u32[]{:S(2)}) copy-start(bf16[2,3,256,256]{3,2,1,0:T(8,128)(2,1)} %param.16) | copy-start | bytes 2359300
  41.6 1.1 copy-start.2
  42.7 2.1 %copy-start.4 = (bf16[8,2,128,256]{3,2,0,1:T(8,128)(2,1)}, bf16[8,2,128,256]{3,2,0,1:T(8,128)(2,1)S(1)}, u32[]{:S(2)}) copy-start(bf16[8,2,128,256]{3,2,0,1:T(8,128)(2,1)S(1)} %get-tuple-element.29) | copy-start | bytes 3145732
  44.8 2.1 %copy-start.6 = (bf16[8,2,128,256]{3,2,0,1:T(8,128)(2,1)}, bf16[8,2,128,256]{3,2,0,1:T(8,128)(2,1)S(1)}, u32[]{:S(2)}) copy-start(bf16[8,2,128,256]{3,2,0,1:T(8,128)(2,1)S(1)} %get-tuple-element.27) | copy-start | bytes 3145732
  47.9 3.7 %copy-start.11 = (f32[1024]{0:T(1024)S(1)}, f32[1024]{0:T(1024)}, u32[]{:S(2)}) copy-start(f32[1024]{0:T(1024)} %param.11) | copy-start | bytes 12292
  47.9 3.8 %copy-start.14 = (f32[3,256]{1,0:T(4,128)S(1)}, f32[3,256]{1,0:T(4,128)}, u32[]{:S(2)}) copy-start(f32[3,256]{1,0:T(4,128)} %param.14) | copy-start | bytes 9220
  47.9 3.8 %copy-start.15 = (s32[16]{0:T(128)S(1)}, s32[16]{0:T(128)}, u32[]{:S(2)}) copy-start(s32[16]{0:T(128)} %param.12) | copy-start | bytes 196
  47.9 29.3 %all-to-all-start.1 = ((bf16[8,2,128,256]{3,2,1,0:T(8,128)(2,1)}), bf16[8,2,128,256]{3,2,1,0:T(8,128)(2,1)S(1)}, u32[]{:S(2)}, u32[]{:S(2)}) async-start(bf16[8,2,128,256]{3,2,1,0:T(8,128)(2,1)} %copy.42), calls=%async_computation.1 | async-start | bytes 2097152 | tf_op jit(solution)/shard_map/all_to_all | solution.py:71
  77.3 3.9 %copy-start.12 = (bf16[4,256]{1,0:T(4,128)(2,1)S(1)}, bf16[4,256]{1,0:T(4,128)(2,1)}, u32[]{:S(2)}) copy-start(bf16[4,256]{1,0:T(4,128)(2,1)} %param.17) | copy-start | bytes 6148
  77.3 5.0 %copy-start.13 = (f32[3,16]{1,0:T(4,128)S(1)}, f32[3,16]{1,0:T(4,128)}, u32[]{:S(2)}) copy-start(f32[3,16]{1,0:T(4,128)} %param.13) | copy-start | bytes 580
  90.7 29.4 %all-to-all-start.2 = ((bf16[8,2,128,256]{3,2,1,0:T(8,128)(2,1)}), bf16[8,2,128,256]{3,2,1,0:T(8,128)(2,1)S(1)}, u32[]{:S(2)}, u32[]{:S(2)}) async-start(bf16[8,2,128,256]{3,2,1,0:T(8,128)(2,1)} %bitcast.190), calls=%async_computation.2 | async-start | bytes 2097152 | tf_op jit(solution)/shard_map/all_to_all | solution.py:84
  94.2 68.6 %reduce-scatter.5.cloned.1.call-start = ((), (), s32[]{:S(2)}) async-start(), calls=%async_computation.6 | async-start | bytes 2359296 | tf_op jit(solution)/shard_map/reduce_scatter | solution.py:106
  120.0 2.3 %copy-start.7 = (bf16[8,2,128,256]{3,2,0,1:T(8,128)(2,1)S(1)}, bf16[8,2,128,256]{3,2,0,1:T(8,128)(2,1)}, u32[]{:S(2)}) copy-start(bf16[8,2,128,256]{3,2,0,1:T(8,128)(2,1)} %get-tuple-element.26) | copy-start | bytes 3145732
  120.0 2.3 %copy-start.10 = (bf16[2,3,256,256]{3,2,1,0:T(8,128)(2,1)S(1)}, bf16[2,3,256,256]{3,2,1,0:T(8,128)(2,1)}, u32[]{:S(2)}) copy-start(bf16[2,3,256,256]{3,2,1,0:T(8,128)(2,1)} %param.16) | copy-start | bytes 2359300
  122.3 1.2 copy-start.1
  122.3 1.5 copy-start.5
  124.5 1.2 copy-start.3
  127.7 37.3 %reduce-scatter.3.cloned.1.call-start = ((), (), s32[]{:S(2)}) async-start(), calls=%async_computation.5 | async-start | bytes 393216 | tf_op jit(solution)/shard_map/reduce_scatter | solution.py:105
  127.7 1.5 copy-start.8
Sparse Core Ops, SparseCore 0:
  127.8 8.1 reduce-scatter.4
  138.9 8.8 reduce-scatter.2
where the time goes:
time: 172 us
  blocking collectives  53.6 us (31%)
  waiting for transfers between devices  50.8 us (30%)
  local copies, waits for them, and re-layouts  19.9 us (12%)
  matrix products  15.8 us (9%)
  between operations  14.3 us (8%)
  other arithmetic  9.77 us (6%)
  starting transfers between devices  7.54 us (4%)
    psum x1, blocking collectives, per_device(): head_grad = lax.psum(head_part, ('expert', 'replica'))  32.1 us
    all_to_all x1, waiting for transfers between devices, per_device(): lax.all_to_all(grad_out, 'expert', split_axis=0, concat_axis=0, tiled=True)  25.6 us
    all_to_all x1, waiting for transfers between devices, per_device(): lax.all_to_all(produced, 'expert', split_axis=0, concat_axis=0, tiled=True)  25.2 us
    all_to_all x1, blocking collectives, per_device(): lax.all_to_all(outbound, 'expert', split_axis=0, concat_axis=0, tiled=True)  21.6 us
    dot_general x4, matrix products, per_device(): jnp.einsum('sxmi,xih->sxmh', current, forward_weight, preferred_element_t...  7.27 us
    scatter x1, local copies, waits for them, and re-layouts, per_device(): jnp.zeros((experts * capacity, hid_width), jnp.bfloat16).at[slot_index]  6.05 us
    dot_general x4, matrix products, per_device(): jnp.einsum('sxmi,sxmh->xih', activations[layer_index], grad_linear, prefe...  4.71 us
    another operation x3, other arithmetic  4.61 us
  transfers between devices with their start and end apart: 4, of which 2 were waited for; matrix products, arithmetic and copies ran while one was open for 3% of the time, Pallas kernels for 0%

commit v1 on v0

v1 whole, which is shorter than its diff:
```python
import functools

import jax
import jax.numpy as jnp
from jax import lax
from jax.experimental import pallas as pl
from jax.experimental.pallas import tpu as pltpu
from jax.sharding import PartitionSpec as P

RAY_SAMPLES = 64
LANES = 128
META = 32
F32 = jnp.float32
BF16 = jnp.bfloat16
VMEM = pltpu.VMEM


def iota(shape, dim):
    return lax.broadcasted_iota(jnp.int32, shape, dim)


def hot(mask, dtype=BF16):
    return jnp.where(mask, 1.0, 0.0).astype(dtype)


def dot(a, b):
    return jnp.dot(a, b, preferred_element_type=F32)


def dot_nt(a, b):
    return lax.dot_general(a, b, (((1,), (1,)), ((), ())), preferred_element_type=F32)


def dot_tn(a, b):
    return lax.dot_general(a, b, (((0,), (0,)), ((), ())), preferred_element_type=F32)


def split(x):
    high = x.astype(BF16)
    return high, (x - high.astype(F32)).astype(BF16)


def lane_row(x):
    return jnp.concatenate([x[k : k + 1] for k in range(x.shape[0])], axis=1)


def ranks(region, experts):
    rows = region.shape[0]
    names = iota((experts, LANES), 0)
    upper = hot(iota((LANES, LANES), 0) <= iota((LANES, LANES), 1))
    equal = [hot(region[k : k + 1] == names, F32) for k in range(rows)]
    running = dot(jnp.concatenate(equal, axis=0).astype(BF16), upper)
    before = jnp.zeros((experts, 1), F32)
    out = []
    for k in range(rows):
        here = running[k * experts : (k + 1) * experts]
        out.append(jnp.sum(equal[k] * (here + before), axis=0, keepdims=True))
        before = before + here[:, LANES - 1 :]
    return jnp.concatenate(out, axis=0).astype(jnp.int32) - 1


def dispatch_kernel(experts, capacity, region_ref, enc_ref, spacing_ref, frame_ref, target_ref, code_ref, out_ref):
    owners, rows = out_ref.shape[0], out_ref.shape[1] - META
    samples = enc_ref.shape[0]
    region = region_ref[...]
    slot = lane_row(region * capacity + ranks(region, experts))
    enc = enc_ref[...]

    chunks = region.shape[0]
    frames = code_ref.shape[1]
    rays = frame_ref.shape[1]
    chosen = hot(frame_ref[...] == iota((frames, rays), 0), F32)
    bias = lax.dot_general(
        code_ref[...], chosen, (((1,), (0,)), ((), ())), precision=lax.Precision.HIGHEST, preferred_element_type=F32
    )
    small = jnp.concatenate([bias, target_ref[...], jnp.zeros((2, rays), F32)], axis=0)
    small_high, small_low = split(small)
    small = jnp.concatenate(
        [small_high.astype(F32), small_low.astype(F32), jnp.zeros((8, LANES - 2 * rays), F32)], axis=1
    )
    spacing_high, spacing_low = split(spacing_ref[...])
    meta = jnp.concatenate(
        [region.astype(F32), spacing_high.astype(F32), spacing_low.astype(F32), small], axis=0
    ).astype(BF16)

    def one(d, carry):
        pick = hot(iota((rows, samples), 0) == slot - d * rows)
        out_ref[d, :rows, :] = dot(pick, enc).astype(BF16)
        out_ref[d, rows:, :] = meta
        return carry

    lax.fori_loop(0, owners, one, 0, unroll=2)


def layer_forward(linear):
    half = jnp.tanh(0.5 * linear)
    gate = 0.5 + 0.5 * half
    act = linear * gate
    slope = gate + act * (1.0 - gate)
    return act.astype(BF16), slope.astype(BF16)


def forward_kernel(capacity, tile, recv_ref, first_ref, hidden_ref, head_ref, act_ref, slope_ref, raw_ref, held):
    sources = recv_ref.shape[0]
    local = first_ref.shape[0]
    layers = hidden_ref.shape[1] + 1
    head = head_ref[...]
    pairs = local * head.shape[0]

    def step(t, carry):
        current = []
        for x in range(local):
            block = recv_ref[pl.ds(t * tile, tile), x * capacity : (x + 1) * capacity, :]
            current.append(block.reshape(tile * capacity, block.shape[2]))
        at = pl.ds(pl.multiple_of(t * tile * capacity, tile * capacity), tile * capacity)
        for layer in range(layers):
            for x in range(local):
                weight = first_ref[x] if layer == 0 else hidden_ref[x, layer - 1]
                act, slope = layer_forward(dot(current[x], weight))
                act_ref[layer, x, at, :] = act
                slope_ref[layer, x, at, :] = slope
                current[x] = act
        raws = [dot_nt(head, current[x]) for x in range(local)]
        for s in range(tile):
            both = jnp.concatenate([r[:, s * capacity : (s + 1) * capacity] for r in raws], axis=0)
            held[pl.ds(pl.multiple_of((t * tile + s) * pairs, pairs), pairs), :] = both
        return carry

    lax.fori_loop(0, sources // tile, step, 0)
    raw = held[...].astype(BF16)
    for d in range(raw_ref.shape[0]):
        raw_ref[d] = raw


def composite(raw, spacing, bias, target):
    row, col = iota((LANES, LANES), 0), iota((LANES, LANES), 1)
    same = row // RAY_SAMPLES == col // RAY_SAMPLES

    def along(x, mask):
        high = x.astype(BF16)
        rest = x - high.astype(F32)
        mid = rest.astype(BF16)
        low = (rest - mid.astype(F32)).astype(BF16)
        w = hot(mask)
        return dot(high, w) + dot(mid, w) + dot(low, w)

    soft = jnp.maximum(raw[0], 0.0) + jnp.log1p(jnp.exp(-jnp.abs(raw[0])))
    optical = soft * spacing
    before = along(optical, same & (row < col))
    reach = jnp.exp(-before)
    left = jnp.exp(-optical)
    weight = reach * (1.0 - left)
    opacity = along(weight, same)
    rendered, graw = [], [None]
    pull = jnp.zeros_like(weight)
    for c in range(1, len(raw)):
        colour = jax.nn.sigmoid(raw[c] + bias[c - 1])
        shade = along(weight * colour, same) + (1.0 - opacity)
        off = shade - target[c - 1]
        rendered.append(shade)
        graw.append(off * weight * colour * (1.0 - colour))
        pull = pull + off * (colour - 1.0)
    optical_pull = pull * reach * left - along(pull * weight, same & (row > col))
    graw[0] = optical_pull * spacing * jax.nn.sigmoid(raw[0])
    return rendered, graw


def render_kernel(
    local, capacity, me_ref, meta_ref, raws_ref, act_ref, head_ref, gslot_ref, headpart_ref, rendered_ref, wide, ranked, dense, grad
):
    owners, pairs = raws_ref.shape[0], raws_ref.shape[1] // meta_ref.shape[0]
    sources = meta_ref.shape[0]
    experts = owners * local
    channels = pairs // local
    me = me_ref[0]
    wide[...] = raws_ref[...].astype(F32)
    samples = ranked.shape[2]
    chunks = samples // LANES
    member = iota((pairs, samples), 0) // channels

    def unslot(s, carry):
        region = meta_ref[s, :chunks, :].astype(F32).astype(jnp.int32)
        rank = lane_row(ranks(region, experts))
        name = lane_row(region)
        pick = hot(iota((capacity, samples), 0) == rank)
        ranked[s] = pick
        at = pl.ds(pl.multiple_of(s * pairs, pairs), pairs)
        block = wide[:, at, :].reshape(owners * pairs, capacity).astype(BF16)
        spread = dot(block, pick)
        total = jnp.zeros((pairs, samples), F32)
        for o in range(owners):
            total = total + jnp.where(name - o * local == member, spread[o * pairs : (o + 1) * pairs], 0.0)
        flat = total[:channels]
        for x in range(1, local):
            flat = flat + total[x * channels : (x + 1) * channels]
        for k in range(chunks):
            for c in range(channels):
                dense[c, pl.ds(s * chunks + k, 1), :] = flat[c : c + 1, k * LANES : (k + 1) * LANES]
        return carry

    lax.fori_loop(0, sources, unslot, 0)

    rays = samples // RAY_SAMPLES
    per_row = rays // chunks
    spacing = (meta_ref[:, chunks : 2 * chunks, :].astype(F32) + meta_ref[:, 2 * chunks : 3 * chunks, :].astype(F32)).reshape(
        sources * chunks, LANES
    )
    small = meta_ref[:, 3 * chunks :, :].astype(F32)
    belongs = iota((chunks, LANES), 1) % rays // per_row == iota((chunks, LANES), 0)
    belongs = belongs & (iota((chunks, LANES), 1) < 2 * rays)
    lay = hot(iota((LANES, LANES), 0) % per_row == iota((LANES, LANES), 1) // RAY_SAMPLES)
    laid = []
    for c in range(2 * (channels - 1)):
        rows = [jnp.where(belongs, small[s, c : c + 1, :], 0.0) for s in range(sources)]
        laid.append(dot(jnp.concatenate(rows, axis=0).astype(BF16), lay))
    shades, graw = composite(
        [dense[c] for c in range(channels)], spacing, laid[: channels - 1], laid[channels - 1 :]
    )
    for c in range(channels):
        grad[c] = graw[c]
    for c in range(channels - 1):
        wide_rows = shades[c].reshape(sources, chunks, LANES)
        mine = jnp.zeros((chunks, LANES), F32)
        for s in range(sources):
            mine = mine + jnp.where(me == s, wide_rows[s], 0.0)
        rendered_ref[c] = mine

    head_total = jnp.zeros((2 * channels, act_ref.shape[2]), F32)

    def slots(s, head_total):
        region = meta_ref[s, :chunks, :].astype(F32).astype(jnp.int32)
        name = lane_row(region)
        at = pl.ds(pl.multiple_of(s * chunks, chunks), chunks)
        flat = jnp.concatenate([lane_row(grad[c, at, :]) for c in range(channels)], axis=0)
        both = jnp.concatenate([flat] * local, axis=0)
        high, low = split(jnp.where(name - me * local == member, both, 0.0))
        got = dot_nt(jnp.concatenate([high, low], axis=0), ranked[s])
        for x in range(local):
            part = jnp.concatenate(
                [got[x * channels : (x + 1) * channels], got[pairs + x * channels : pairs + (x + 1) * channels]], axis=0
            ).astype(BF16)
            gslot_ref[x, s] = part
            feature = act_ref[x, pl.ds(pl.multiple_of(s * capacity, capacity), capacity), :]
            head_total = head_total + dot(part, feature)
        return head_total

    head_total = lax.fori_loop(0, sources, slots, head_total)
    part = head_total[:channels] + head_total[channels:]
    for d in range(headpart_ref.shape[0]):
        headpart_ref[d] = part


def backward_kernel(
    capacity, copies, me_ref, recv_ref, act_ref, slope_ref, gslot_ref, first_ref, hidden_ref, head_ref, *rest
):
    outs, (gfirst, ghidden) = rest[: 2 * copies], rest[2 * copies :]
    local, sources = gslot_ref.shape[0], gslot_ref.shape[1]
    layers = hidden_ref.shape[1] + 1
    head = head_ref[...]
    head = jnp.concatenate([head, head], axis=0)
    rows = sources * capacity
    up = []
    for x in range(local):
        pieces = [dot_tn(gslot_ref[x, s], head) for s in range(sources)]
        up.append(jnp.concatenate(pieces, axis=0).astype(BF16))
    for layer in reversed(range(layers)):
        for x in range(local):
            glin = up[x] * slope_ref[layer, x]
            if layer:
                ghidden[x, layer - 1] = dot_tn(act_ref[layer - 1, x], glin)
                up[x] = dot_nt(glin, hidden_ref[x, layer - 1]).astype(BF16)
            else:
                block = recv_ref[:, x * capacity : (x + 1) * capacity, :].reshape(rows, recv_ref.shape[2])
                gfirst[x] = dot_tn(block, glin)
    me = me_ref[0]
    for s in range(copies):
        first_out, hidden_out = outs[2 * s], outs[2 * s + 1]
        piece = lax.rem(me + s, copies)
        size = first_out.shape[1]
        first_out[...] = gfirst[:, pl.ds(pl.multiple_of(piece * size, size), size), :]
        size = hidden_out.shape[2]
        hidden_out[...] = ghidden[:, :, pl.ds(pl.multiple_of(piece * size, size), size), :]


def shape(dims, dtype):
    return jax.ShapeDtypeStruct(dims, dtype)


def call(kernel, outs, ins, scratch=(), scalars=0):
    specs = [pl.BlockSpec(memory_space=pltpu.SMEM)] * scalars
    specs += [pl.BlockSpec(memory_space=VMEM)] * (len(ins) - scalars)
    return pl.pallas_call(
        kernel,
        out_shape=outs,
        in_specs=specs,
        out_specs=[pl.BlockSpec(memory_space=VMEM)] * len(outs),
        scratch_shapes=list(scratch),
        compiler_params=pltpu.CompilerParams(vmem_limit_bytes=48 * 1024 * 1024),
    )(*ins)


def per_device(
    encoded, region_id, spacing, frame_index, target_rgb, frame_code, first_weight, hidden_weight, head_weight
):
    owners, copies = lax.axis_size("expert"), lax.axis_size("replica")
    local = first_weight.shape[0]
    experts = owners * local
    samples, enc_width = encoded.shape
    capacity = 2 * samples // experts
    hid = first_weight.shape[2]
    layers = hidden_weight.shape[1] + 1
    channels = head_weight.shape[0]
    chunks = samples // LANES
    slots = local * capacity
    rows = owners * capacity
    owner = lax.axis_index("expert").astype(jnp.int32).reshape(1)
    copy = lax.axis_index("replica").astype(jnp.int32).reshape(1)

    (outbound,) = call(
        functools.partial(dispatch_kernel, experts, capacity),
        [shape((owners, slots + META, enc_width), BF16)],
        [
            region_id.reshape(chunks, LANES),
            encoded,
            spacing.reshape(chunks, LANES),
            frame_index.reshape(1, -1),
            target_rgb,
            frame_code,
        ],
    )
    recv = lax.all_to_all(outbound, "expert", split_axis=0, concat_axis=0, tiled=True)
    rows_out = owners * local * channels
    acts, slopes, raw = call(
        functools.partial(forward_kernel, capacity, 2),
        [
            shape((layers, local, rows, hid), BF16),
            shape((layers, local, rows, hid), BF16),
            shape((owners, rows_out, capacity), BF16),
        ],
        [recv, first_weight, hidden_weight, head_weight],
        [pltpu.VMEM((rows_out, capacity), F32)],
    )
    raws = lax.all_to_all(raw, "expert", split_axis=0, concat_axis=0, tiled=True)
    meta = recv[:, slots:, :]
    gslot, headpart, rendered = call(
        functools.partial(render_kernel, local, capacity),
        [
            shape((local, owners, 2 * channels, capacity), BF16),
            shape((owners * copies, channels, hid), F32),
            shape((channels - 1, chunks, LANES), F32),
        ],
        [owner, meta, raws, acts[layers - 1], head_weight],
        [
            pltpu.VMEM((owners, owners * local * channels, capacity), F32),
            pltpu.VMEM((owners, capacity, samples), BF16),
            pltpu.VMEM((channels, owners * chunks, LANES), F32),
            pltpu.VMEM((channels, owners * chunks, LANES), F32),
        ],
        scalars=1,
    )
    heads = lax.all_to_all(headpart, ("expert", "replica"), split_axis=0, concat_axis=0, tiled=True)
    pieces = []
    for _ in range(copies):
        pieces.append(shape((local, enc_width // copies, hid), F32))
        pieces.append(shape((local, layers - 1, hid // copies, hid), F32))
    grads = call(
        functools.partial(backward_kernel, capacity, copies),
        pieces,
        [copy, recv, acts, slopes, gslot, first_weight, hidden_weight, head_weight],
        [pltpu.VMEM(first_weight.shape, F32), pltpu.VMEM(hidden_weight.shape, F32)],
        scalars=1,
    )
    first_grad, hidden_grad = grads[0], grads[1]
    for s in range(1, copies):
        ring = [(i, (i + s) % copies) for i in range(copies)]
        first_grad = first_grad + lax.ppermute(grads[2 * s], "replica", ring)
        hidden_grad = hidden_grad + lax.ppermute(grads[2 * s + 1], "replica", ring)
    head_grad = jnp.sum(heads, axis=0)
    rendered = rendered[:, :, ::RAY_SAMPLES].reshape(channels - 1, -1)
    return (first_grad, hidden_grad, head_grad, rendered)


def solution(mesh):
    placed = (
        P(("groups", "expert", "replica"), None),
        P(("groups", "expert", "replica")),
        P(("groups", "expert", "replica")),
        P(("groups", "expert", "replica")),
        P(None, ("groups", "expert", "replica")),
        P(None, "groups"),
        P("expert", None, None),
        P("expert", None, None, None),
        P(),
    )
    return jax.shard_map(
        per_device,
        mesh=mesh,
        in_specs=placed,
        out_specs=(
            P(("groups", "expert"), "replica", None),
            P(("groups", "expert"), None, "replica", None),
            P("groups", None),
            P(None, ("groups", "expert", "replica")),
        ),
        check_vma=False,
    )
```

time: 172 us -> 80.2 us (0.47)
  blocking collectives: 53.6 us -> 0 us
  waiting for transfers between devices: 50.8 us -> 28.1 us
  Pallas kernels: 0 us -> 22.4 us
  matrix products: 15.8 us -> 0 us
  between operations: 14.3 us -> 0.7 us
  local copies, waits for them, and re-layouts: 19.9 us -> 11.2 us
  other arithmetic: 9.77 us -> 2.27 us
  starting transfers between devices: 7.54 us -> 15 us
    psum x1 -> x0, blocking collectives: 32.1 us -> none  [per_device(): head_grad = lax.psum(head_part, ('expert', 'replica'))]
    all_to_all x2 -> x3, waiting for transfers between devices: 50.8 us -> 28 us  [the longest x1 15.9 us: per_device(): lax.all_to_all(outbound, 'expert', split_axis=0, concat_axis=0, tiled=True)]
    pallas_call x0 -> x4, Pallas kernels: none -> 22.4 us  [call(): pl.pallas_call(kernel, out_shape=outs, in_specs=specs, out_specs=[pl.Bloc...]
    all_to_all x1 -> x0, blocking collectives: 21.6 us -> none  [per_device(): lax.all_to_all(outbound, 'expert', split_axis=0, concat_axis=0, tiled=True)]
    dot_general x15 -> x0, matrix products: 15.8 us -> none  [the longest x4 7.27 us: per_device(): jnp.einsum('sxmi,xih->sxmh', current, forward_weight, preferred_element_t...]
    scatter x2 -> x0, local copies, waits for them, and re-layouts: 9.73 us -> none  [the longest x1 6.05 us: per_device(): jnp.zeros((experts * capacity, hid_width), jnp.bfloat16).at[slot_index]]
    all_to_all x2 -> x3, starting transfers between devices: 7.28 us -> 14.4 us  [the longest x1 7.25 us: per_device(): lax.all_to_all(outbound, 'expert', split_axis=0, concat_axis=0, tiled=True)]
    another operation x6 -> x0, other arithmetic: 6.54 us -> none
  transfers between devices with their start and end apart: 4 -> 5, of which waited for: 2 -> 3; matrix products, arithmetic and copies ran while one was open for 3% -> 4% of each run, Pallas kernels for 0% -> 0%
where the time goes in v1:
time: 80.2 us; the launch traced here: 79.5 us
  waiting for transfers between devices  28.1 us (35%)
  Pallas kernels  22.4 us (28%)
  starting transfers between devices  15 us (19%)
  local copies, waits for them, and re-layouts  11.2 us (14%)
  other arithmetic  2.27 us (3%)
    pallas_call x4, Pallas kernels, call(): pl.pallas_call(kernel, out_shape=outs, in_specs=specs, out_specs=[pl.Bloc...  22.4 us
    all_to_all x1, waiting for transfers between devices, per_device(): lax.all_to_all(outbound, 'expert', split_axis=0, concat_axis=0, tiled=True)  15.9 us
    unnamed x26, local copies, waits for them, and re-layouts  9.14 us
    all_to_all x1, starting transfers between devices, per_device(): lax.all_to_all(outbound, 'expert', split_axis=0, concat_axis=0, tiled=True)  7.25 us
    all_to_all x1, waiting for transfers between devices, per_device(): lax.all_to_all(headpart, ('expert', 'replica'), split_axis=0, concat_axis...  6.12 us
    all_to_all x1, waiting for transfers between devices, per_device(): lax.all_to_all(raw, 'expert', split_axis=0, concat_axis=0, tiled=True)  6.04 us
    all_to_all x1, starting transfers between devices, per_device(): lax.all_to_all(raw, 'expert', split_axis=0, concat_axis=0, tiled=True)  3.64 us
    all_to_all x1, starting transfers between devices, per_device(): lax.all_to_all(headpart, ('expert', 'replica'), split_axis=0, concat_axis...  3.5 us
  transfers between devices with their start and end apart: 5, of which 3 were waited for; matrix products, arithmetic and copies ran while one was open for 4% of the time, Pallas kernels for 0%

profile of v1, /device:TPU:0, one launch (start us, length us, event | category | flops | bytes accessed | tf_op | source)
XLA Modules:
  0.0 79.5 jit_solution(12100897095158410427)
XLA Ops:
  0.6 0.0 copy-start.2
  0.6 0.0 copy-start.4
  0.7 0.0 copy-start.5
  0.7 1.0 %copy-done.5 = bf16[1024,128]{1,0:T(8,128)(2,1)S(1)} copy-done((bf16[1024,128]{1,0:T(8,128)(2,1)S(1)}, bf16[1024,128]{1,0:T(8,128)(2,1)}, u32[]{:S(2)}) %copy-start.5) | copy-done | bytes 262168
  1.7 0.0 copy-start.8
  1.7 0.7 copy-done.8
  2.4 0.0 copy-start.9
  2.4 0.7 copy-done.9
  3.1 0.0 copy-start.10
  3.1 0.7 copy-done.10
  3.7 0.0 copy-start.11
  3.7 0.7 copy-done.11
  4.4 0.0 copy-start.12
  4.4 0.7 copy-done.12
  5.1 0.0 copy-start.7
  5.1 2.8 %shard_map.120 = bf16[8,288,128]{2,1,0:T(8,128)(2,1)} custom-call(s32[8,128]{1,0:T(8,128)S(1)} %bitcast.7, bf16[1024,128]{1,0:T(8,128)(2,1)S(1)} %copy-done.5, f32[8,128]{1,0:T(8,128)S(1)} %bitcast.8, s32[1,16]{1,0:T(1,128)S(1)} %bitcast.9, f32[3,16]{1,0:T(4,128)S(1)} %copy-done.11, f32[3,256]{1,0:T(4,128)S(1)} %copy-done.10), custom_call_target="tpu_custom_call" | custom-call | tf_op jit(solution)/shard_map/pallas_call | solution.py:292
  7.9 7.2 %all-to-all-start = ((bf16[8,288,128]{2,1,0:T(8,128)(2,1)}), bf16[8,288,128]{2,1,0:T(8,128)(2,1)S(1)}, u32[]{:S(2)}, u32[]{:S(2)}) async-start(bf16[8,288,128]{2,1,0:T(8,128)(2,1)} %shard_map.120), calls=%async_computation | async-start | bytes 1179648 | tf_op jit(solution)/shard_map/all_to_all | solution.py:331
  15.2 15.9 %all-to-all-done.recv_ref = bf16[8,288,128]{2,1,0:T(8,128)(2,1)S(1)} async-done(((bf16[8,288,128]{2,1,0:T(8,128)(2,1)}), bf16[8,288,128]{2,1,0:T(8,128)(2,1)S(1)}, u32[]{:S(2)}, u32[]{:S(2)}) %all-to-all-start) | async-done | bytes 589856 | tf_op jit(solution)/shard_map/all_to_all | solution.py:331
  31.1 0.0 copy-start.1
  31.1 1.1 %copy-done.1 = bf16[2,3,256,256]{3,2,1,0:T(8,128)(2,1)S(1)} copy-done((bf16[2,3,256,256]{3,2,1,0:T(8,128)(2,1)S(1)}, bf16[2,3,256,256]{3,2,1,0:T(8,128)(2,1)}, u32[]{:S(2)}) %copy-start.1) | copy-done | bytes 786456
  32.2 0.0 copy-start.3
  32.2 0.9 %copy-done.3 = bf16[2,128,256]{2,1,0:T(8,128)(2,1)S(1)} copy-done((bf16[2,128,256]{2,1,0:T(8,128)(2,1)S(1)}, bf16[2,128,256]{2,1,0:T(8,128)(2,1)}, u32[]{:S(2)}) %copy-start.3) | copy-done | bytes 131096
  33.1 0.0 copy-start.6
  33.1 0.7 copy-done.6
  33.8 5.9 %shard_map.121 = (bf16[4,2,1024,256]{3,2,1,0:T(8,128)(2,1)S(1)}, bf16[4,2,1024,256]{3,2,1,0:T(8,128)(2,1)}, bf16[8,64,128]{2,1,0:T(8,128)(2,1)}) custom-call(bf16[8,288,128]{2,1,0:T(8,128)(2,1)S(1)} %all-to-all-done.recv_ref, bf16[2,128,256]{2,1,0:T(8,128)(2,1)S(1)} %copy-done.3, bf16[2,3,256,256]{3,2,1,0:T(8,128)(2,1)S(1)} %copy-done.1, ...), custom_call_target="tpu_custom_call" | custom-call | tf_op jit(solution)/shard_map/pallas_call | solution.py:292
  39.6 0.0 copy-start
  39.6 2.0 %copy-done = bf16[4,2,1024,256]{3,2,1,0:T(8,128)(2,1)} copy-done((bf16[4,2,1024,256]{3,2,1,0:T(8,128)(2,1)}, bf16[4,2,1024,256]{3,2,1,0:T(8,128)(2,1)S(1)}, u32[]{:S(2)}) %copy-start) | copy-done | bytes 4194328
  41.6 3.6 %all-to-all-start.1 = ((bf16[8,64,128]{2,1,0:T(8,128)(2,1)}), bf16[8,64,128]{2,1,0:T(8,128)(2,1)S(1)}, u32[]{:S(2)}, u32[]{:S(2)}) async-start(bf16[8,64,128]{2,1,0:T(8,128)(2,1)} %get-tuple-element.16), calls=%async_computation.1 | async-start | bytes 262144 | tf_op jit(solution)/shard_map/all_to_all | solution.py:343
  45.3 1.3 %slice_bitcast_fusion.act_ref = bf16[2,1024,256]{2,1,0:T(8,128)(2,1)S(1)} fusion(bf16[4,2,1024,256]{3,2,1,0:T(8,128)(2,1)} %copy-done), kind=kLoop, calls=%fused_computation | loop fusion | bytes 2097152 | tf_op jit(solution)/shard_map/squeeze | solution.py:352
  46.6 6.0 %all-to-all-done.1.raws_ref = bf16[8,64,128]{2,1,0:T(8,128)(2,1)S(1)} async-done(((bf16[8,64,128]{2,1,0:T(8,128)(2,1)}), bf16[8,64,128]{2,1,0:T(8,128)(2,1)S(1)}, u32[]{:S(2)}, u32[]{:S(2)}) %all-to-all-start.1) | async-done | bytes 131104 | tf_op jit(solution)/shard_map/all_to_all | solution.py:343
  52.6 0.0 copy-done.7
  52.6 7.6 %shard_map.122 = (bf16[2,8,8,128]{3,2,1,0:T(8,128)(2,1)S(1)}, f32[16,4,256]{2,1,0:T(4,128)}, f32[3,8,128]{2,1,0:T(8,128)S(1)}) custom-call(s32[1]{0:T(128)} %bitcast.4.me_ref, bf16[8,32,128]{2,1,0:T(8,128)(2,1)S(1)} %slice.12.meta_ref, bf16[8,64,128]{2,1,0:T(8,128)(2,1)S(1)} %all-to-all-done.1.raws_ref, bf16[2,1024,256]{2,1,0:T(8,128)(2,1)S(1)} %slice_bitcast_fusion.act_ref, ...), custom_call_target="tpu_custom_call" | custom-call | tf_op jit(solution)/shard_map/pallas_call | solution.py:292
  60.2 0.0 copy-done.2
  60.2 0.0 copy-done.4
  60.2 6.1 %shard_map.123 = (f32[2,64,256]{2,1,0:T(8,128)S(1)}, f32[2,3,128,256]{3,2,1,0:T(8,128)S(1)}, f32[2,64,256]{2,1,0:T(8,128)S(1)}, f32[2,3,128,256]{3,2,1,0:T(8,128)S(1)}) custom-call(s32[1]{0:T(128)} %bitcast.me_ref, bf16[8,288,128]{2,1,0:T(8,128)(2,1)S(1)} %all-to-all-done.recv_ref, bf16[4,2,1024,256]{3,2,1,0:T(8,128)(2,1)} %copy-done, ...), custom_call_target="tpu_custom_call" | custom-call | tf_op jit(solution)/shard_map/pallas_call | solution.py:292
  66.3 0.1 collective-permute-start.1
  66.4 0.5 collective-permute-start
  66.9 3.5 %all-to-all-start.2 = ((f32[16,4,256]{2,1,0:T(4,128)}), f32[16,4,256]{2,1,0:T(4,128)S(1)}, u32[]{:S(2)}, u32[]{:S(2)}) async-start(f32[16,4,256]{2,1,0:T(4,128)} %get-tuple-element.22), calls=%async_computation.2 | async-start | bytes 131072 | tf_op jit(solution)/shard_map/all_to_all | solution.py:361
  70.4 0.1 slice.11
  70.5 0.7 reshape.31
  71.1 6.1 %all-to-all-done.2 = f32[16,4,256]{2,1,0:T(4,128)S(1)} async-done(((f32[16,4,256]{2,1,0:T(4,128)}), f32[16,4,256]{2,1,0:T(4,128)S(1)}, u32[]{:S(2)}, u32[]{:S(2)}) %all-to-all-start.2) | async-done | bytes 65568 | tf_op jit(solution)/shard_map/all_to_all | solution.py:361
  77.2 0.6 reduce_sum.9
  77.9 0.0 collective-permute-done
  77.9 0.7 add.6
  78.5 0.0 collective-permute-done.1
  78.5 1.0 %add.7 = f32[2,3,128,256]{3,2,1,0:T(8,128)} add(f32[2,3,128,256]{3,2,1,0:T(8,128)S(1)} %get-tuple-element.20, f32[2,3,128,256]{3,2,1,0:T(8,128)S(1)} %collective-permute-done.1) | non-fusion elementwise | flops 196608 | bytes 2359296 | tf_op jit(solution)/shard_map/add | solution.py:377
  (1 shorter events, 0.0 us)
Async XLA Ops:
  0.6 59.6 %copy-start.2 = (bf16[2,3,256,256]{3,2,1,0:T(8,128)(2,1)S(1)}, bf16[2,3,256,256]{3,2,1,0:T(8,128)(2,1)}, u32[]{:S(2)}) copy-start(bf16[2,3,256,256]{3,2,1,0:T(8,128)(2,1)} %hidden_ref.3) | copy-start | bytes 2359300
  0.6 59.6 %copy-start.4 = (bf16[2,128,256]{2,1,0:T(8,128)(2,1)S(1)}, bf16[2,128,256]{2,1,0:T(8,128)(2,1)}, u32[]{:S(2)}) copy-start(bf16[2,128,256]{2,1,0:T(8,128)(2,1)} %first_ref.3) | copy-start | bytes 393220
  0.7 1.0 %copy-start.5 = (bf16[1024,128]{1,0:T(8,128)(2,1)S(1)}, bf16[1024,128]{1,0:T(8,128)(2,1)}, u32[]{:S(2)}) copy-start(bf16[1024,128]{1,0:T(8,128)(2,1)} %enc_ref.1) | copy-start | bytes 786436
  1.7 0.7 copy-start.8
  2.4 0.7 copy-start.9
  3.1 0.7 copy-start.10
  3.7 0.7 copy-start.11
  4.4 0.7 copy-start.12
  5.1 47.5 %copy-start.7 = (bf16[4,256]{1,0:T(4,128)(2,1)S(1)}, bf16[4,256]{1,0:T(4,128)(2,1)}, u32[]{:S(2)}) copy-start(bf16[4,256]{1,0:T(4,128)(2,1)} %head_ref.5) | copy-start | bytes 6148
  7.9 23.1 %all-to-all-start = ((bf16[8,288,128]{2,1,0:T(8,128)(2,1)}), bf16[8,288,128]{2,1,0:T(8,128)(2,1)S(1)}, u32[]{:S(2)}, u32[]{:S(2)}) async-start(bf16[8,288,128]{2,1,0:T(8,128)(2,1)} %shard_map.120), calls=%async_computation | async-start | bytes 1179648 | tf_op jit(solution)/shard_map/all_to_all | solution.py:331
  31.1 1.1 %copy-start.1 = (bf16[2,3,256,256]{3,2,1,0:T(8,128)(2,1)S(1)}, bf16[2,3,256,256]{3,2,1,0:T(8,128)(2,1)}, u32[]{:S(2)}) copy-start(bf16[2,3,256,256]{3,2,1,0:T(8,128)(2,1)} %hidden_ref.3) | copy-start | bytes 2359300
  32.2 0.9 %copy-start.3 = (bf16[2,128,256]{2,1,0:T(8,128)(2,1)S(1)}, bf16[2,128,256]{2,1,0:T(8,128)(2,1)}, u32[]{:S(2)}) copy-start(bf16[2,128,256]{2,1,0:T(8,128)(2,1)} %first_ref.3) | copy-start | bytes 393220
  33.1 0.7 copy-start.6
  39.6 2.0 %copy-start = (bf16[4,2,1024,256]{3,2,1,0:T(8,128)(2,1)}, bf16[4,2,1024,256]{3,2,1,0:T(8,128)(2,1)S(1)}, u32[]{:S(2)}) copy-start(bf16[4,2,1024,256]{3,2,1,0:T(8,128)(2,1)S(1)} %get-tuple-element.14.act_ref) | copy-start | bytes 12582916
  41.6 11.0 %all-to-all-start.1 = ((bf16[8,64,128]{2,1,0:T(8,128)(2,1)}), bf16[8,64,128]{2,1,0:T(8,128)(2,1)S(1)}, u32[]{:S(2)}, u32[]{:S(2)}) async-start(bf16[8,64,128]{2,1,0:T(8,128)(2,1)} %get-tuple-element.16), calls=%async_computation.1 | async-start | bytes 262144 | tf_op jit(solution)/shard_map/all_to_all | solution.py:343
  66.3 12.2 %collective-permute-start.1 = (f32[2,3,128,256]{3,2,1,0:T(8,128)S(1)}, f32[2,3,128,256]{3,2,1,0:T(8,128)S(1)}, u32[]{:S(2)}, u32[]{:S(2)}) collective-permute-start(f32[2,3,128,256]{3,2,1,0:T(8,128)S(1)} %get-tuple-element.21), channel_id=1, source_target_pairs={{0,1},{1,0},{2,3},{3,2},{4,5},{5,4},{6,7},{7,6},{8,9},{9,8},{10,11... | collective-permute-start | bytes 2359304 | tf_op jit(solution)/shard_map/ppermute | solution.py:377
  66.4 11.5 %collective-permute-start = (f32[2,64,256]{2,1,0:T(8,128)S(1)}, f32[2,64,256]{2,1,0:T(8,128)S(1)}, u32[]{:S(2)}, u32[]{:S(2)}) collective-permute-start(f32[2,64,256]{2,1,0:T(8,128)S(1)} %get-tuple-element.19), channel_id=1, source_target_pairs={{0,1},{1,0},{2,3},{3,2},{4,5},{5,4},{6,7},{7,6},{8,9},{9,8},{10,11... | collective-permute-start | bytes 393224 | tf_op jit(solution)/shard_map/ppermute | solution.py:376
  66.9 10.4 %all-to-all-start.2 = ((f32[16,4,256]{2,1,0:T(4,128)}), f32[16,4,256]{2,1,0:T(4,128)S(1)}, u32[]{:S(2)}, u32[]{:S(2)}) async-start(f32[16,4,256]{2,1,0:T(4,128)} %get-tuple-element.22), calls=%async_computation.2 | async-start | bytes 131072 | tf_op jit(solution)/shard_map/all_to_all | solution.py:361

commit v2 on v1

v2 whole, which is shorter than its diff:
```python
import functools

import jax
import jax.numpy as jnp
from jax import lax
from jax.experimental import pallas as pl
from jax.experimental.pallas import tpu as pltpu
from jax.sharding import PartitionSpec as P

RAY_SAMPLES = 64
LANES = 128
META = 32
F32 = jnp.float32
BF16 = jnp.bfloat16
VMEM = pltpu.VMEM


def iota(shape, dim):
    return lax.broadcasted_iota(jnp.int32, shape, dim)


def hot(mask, dtype=BF16):
    return jnp.where(mask, 1.0, 0.0).astype(dtype)


def dot(a, b):
    return jnp.dot(a, b, preferred_element_type=F32)


def dot_nt(a, b):
    return lax.dot_general(a, b, (((1,), (1,)), ((), ())), preferred_element_type=F32)


def dot_tn(a, b):
    return lax.dot_general(a, b, (((0,), (0,)), ((), ())), preferred_element_type=F32)


def split(x):
    high = x.astype(BF16)
    return high, (x - high.astype(F32)).astype(BF16)


def lane_row(x):
    return jnp.concatenate([x[k : k + 1] for k in range(x.shape[0])], axis=1)


def ranks(region, experts):
    rows = region.shape[0]
    names = iota((experts, LANES), 0)
    upper = hot(iota((LANES, LANES), 0) <= iota((LANES, LANES), 1))
    equal = [hot(region[k : k + 1] == names, F32) for k in range(rows)]
    running = dot(jnp.concatenate(equal, axis=0).astype(BF16), upper)
    before = jnp.zeros((experts, 1), F32)
    out = []
    for k in range(rows):
        here = running[k * experts : (k + 1) * experts]
        out.append(jnp.sum(equal[k] * (here + before), axis=0, keepdims=True))
        before = before + here[:, LANES - 1 :]
    return jnp.concatenate(out, axis=0).astype(jnp.int32) - 1


def dispatch_kernel(experts, capacity, *refs):
    outside, (out_ref, first_out, hidden_out, head_out), refs = refs[:9], refs[9:13], refs[13:]
    inside, (held, loaded, sent) = refs[:9], refs[9:]
    loads = [pltpu.make_async_copy(a, b, loaded.at[i]) for i, (a, b) in enumerate(zip(outside, inside))]
    for load in loads:
        load.start()
    region_ref, enc_ref, spacing_ref, frame_ref, target_ref, code_ref, first_ref, hidden_ref, head_ref = inside
    owners, rows = held.shape[0], held.shape[1] - META
    samples = enc_ref.shape[0]
    for load in loads[:6]:
        load.wait()
    region = region_ref[...]
    slot = lane_row(region * capacity + ranks(region, experts))
    enc = enc_ref[...]

    frames = code_ref.shape[1]
    rays = frame_ref.shape[1]
    chosen = hot(frame_ref[...] == iota((frames, rays), 0), F32)
    bias = lax.dot_general(
        code_ref[...], chosen, (((1,), (0,)), ((), ())), precision=lax.Precision.HIGHEST, preferred_element_type=F32
    )
    small = jnp.concatenate([bias, target_ref[...], jnp.zeros((2, rays), F32)], axis=0)
    small_high, small_low = split(small)
    small = jnp.concatenate(
        [small_high.astype(F32), small_low.astype(F32), jnp.zeros((8, LANES - 2 * rays), F32)], axis=1
    )
    spacing_high, spacing_low = split(spacing_ref[...])
    meta = jnp.concatenate(
        [region.astype(F32), spacing_high.astype(F32), spacing_low.astype(F32), small], axis=0
    ).astype(BF16)

    def send(d):
        return pltpu.make_async_copy(held.at[d], out_ref.at[d], sent.at[d])

    def one(d, carry):
        pick = hot(iota((rows, samples), 0) == slot - d * rows)
        held[d, :rows, :] = dot(pick, enc).astype(BF16)
        held[d, rows:, :] = meta
        send(d).start()
        return carry

    lax.fori_loop(0, owners, one, 0, unroll=2)
    for load in loads[6:]:
        load.wait()
    first_out[...] = first_ref[...] * 0.5
    hidden_out[...] = hidden_ref[...] * 0.5
    head_out[...] = head_ref[...]

    def finish(d, carry):
        send(d).wait()
        return carry

    lax.fori_loop(0, owners, finish, 0)


def layer_forward(half):
    t = jnp.tanh(half)
    p = half * t
    return (half + p).astype(BF16), ((1.0 + t) * (1.0 + (half - p))).astype(BF16)


def forward_kernel(
    capacity, tile, recv_ref, first_ref, hidden_ref, head_ref, act_out, slope_out, raw_ref, top_ref, held, act_ref, slope_ref, done
):
    sources = recv_ref.shape[0]
    local = first_ref.shape[0]
    layers = hidden_ref.shape[1] + 1
    head = head_ref[...]
    pairs = local * head.shape[0]

    def saves(t):
        at = pl.ds(pl.multiple_of(t * tile * capacity, tile * capacity), tile * capacity)
        return (
            pltpu.make_async_copy(act_ref.at[:, :, at, :], act_out.at[:, :, at, :], done.at[0, t]),
            pltpu.make_async_copy(slope_ref.at[:, :, at, :], slope_out.at[:, :, at, :], done.at[1, t]),
        )

    def step(t, carry):
        current = []
        for x in range(local):
            block = recv_ref[pl.ds(t * tile, tile), x * capacity : (x + 1) * capacity, :]
            current.append(block.reshape(tile * capacity, block.shape[2]))
        at = pl.ds(pl.multiple_of(t * tile * capacity, tile * capacity), tile * capacity)
        for layer in range(layers):
            for x in range(local):
                weight = first_ref[x] if layer == 0 else hidden_ref[x, layer - 1]
                act, slope = layer_forward(dot(current[x], weight))
                if layer < layers - 1:
                    act_ref[layer, x, at, :] = act
                else:
                    top_ref[x, at, :] = act
                slope_ref[layer, x, at, :] = slope
                current[x] = act
        raws = [dot_nt(head, current[x]) for x in range(local)]
        for s in range(tile):
            both = jnp.concatenate([r[:, s * capacity : (s + 1) * capacity] for r in raws], axis=0)
            held[pl.ds(pl.multiple_of((t * tile + s) * pairs, pairs), pairs), :] = both
        for save in saves(t):
            save.start()
        return carry

    lax.fori_loop(0, sources // tile, step, 0)
    raw = held[...].astype(BF16)
    for d in range(raw_ref.shape[0]):
        raw_ref[d] = raw

    def finish(t, carry):
        for save in saves(t):
            save.wait()
        return carry

    lax.fori_loop(0, sources // tile, finish, 0)


def composite(raw, spacing, bias, target):
    row, col = iota((LANES, LANES), 0), iota((LANES, LANES), 1)
    same = row // RAY_SAMPLES == col // RAY_SAMPLES

    def along(x, mask):
        high = x.astype(BF16)
        rest = x - high.astype(F32)
        mid = rest.astype(BF16)
        low = (rest - mid.astype(F32)).astype(BF16)
        w = hot(mask)
        return dot(high, w) + dot(mid, w) + dot(low, w)

    soft = jnp.maximum(raw[0], 0.0) + jnp.log1p(jnp.exp(-jnp.abs(raw[0])))
    optical = soft * spacing
    before = along(optical, same & (row < col))
    reach = jnp.exp(-before)
    left = jnp.exp(-optical)
    weight = reach * (1.0 - left)
    opacity = along(weight, same)
    rendered, graw = [], [None]
    pull = jnp.zeros_like(weight)
    for c in range(1, len(raw)):
        colour = jax.nn.sigmoid(raw[c] + bias[c - 1])
        shade = along(weight * colour, same) + (1.0 - opacity)
        off = shade - target[c - 1]
        rendered.append(shade)
        graw.append(off * weight * colour * (1.0 - colour))
        pull = pull + off * (colour - 1.0)
    optical_pull = pull * reach * left - along(pull * weight, same & (row > col))
    graw[0] = optical_pull * spacing * jax.nn.sigmoid(raw[0])
    return rendered, graw


def plan_kernel(
    local, capacity, act_in, recv_ref, actt_out, rank_ref, name_ref, laid_ref, enct_ref, act_ref, actt_ref, moved
):
    layers = actt_ref.shape[0]
    loads = [pltpu.make_async_copy(act_in.at[k], act_ref.at[k], moved.at[0, k]) for k in range(layers)]
    saves = [pltpu.make_async_copy(actt_ref.at[k], actt_out.at[k], moved.at[1, k]) for k in range(layers)]
    for load in loads:
        load.start()
    sources, slots = recv_ref.shape[0], recv_ref.shape[1] - META
    rows = sources * capacity
    experts = sources * local
    samples = rank_ref.shape[2]
    chunks = samples // LANES

    def one(s, carry):
        region = recv_ref[s, slots : slots + chunks, :].astype(F32).astype(jnp.int32)
        rank_ref[s] = jnp.broadcast_to(lane_row(ranks(region, experts)), (8, samples))
        name_ref[s] = jnp.broadcast_to(lane_row(region), (8, samples))
        return carry

    lax.fori_loop(0, sources, one, 0, unroll=2)

    rays = samples // RAY_SAMPLES
    per_row = rays // chunks
    meta = recv_ref[:, slots:, :].astype(F32)
    laid_ref[0] = (meta[:, chunks : 2 * chunks] + meta[:, 2 * chunks : 3 * chunks]).reshape(sources * chunks, LANES)
    small = meta[:, 3 * chunks :]
    lane = iota((chunks, LANES), 1)
    belongs = (lane % rays // per_row == iota((chunks, LANES), 0)) & (lane < 2 * rays)
    lay = hot(iota((LANES, LANES), 0) % per_row == iota((LANES, LANES), 1) // RAY_SAMPLES)
    for c in range(laid_ref.shape[0] - 1):
        parts = [jnp.where(belongs, small[s, c : c + 1, :], 0.0) for s in range(sources)]
        laid_ref[1 + c] = dot(jnp.concatenate(parts, axis=0).astype(BF16), lay)

    for x in range(local):
        enct_ref[x] = recv_ref[:, x * capacity : (x + 1) * capacity, :].reshape(rows, recv_ref.shape[2]).T
    for layer in reversed(range(layers)):
        loads[layer].wait()
        for x in range(local):
            actt_ref[layer, x] = act_ref[layer, x].T
        saves[layer].start()
    for save in saves:
        save.wait()


def render_kernel(
    local,
    capacity,
    me_ref,
    act_ref,
    raws_ref,
    rank_ref,
    name_ref,
    laid_ref,
    gslot_ref,
    headpart_ref,
    rendered_ref,
    wide,
    dense,
    grad,
    ranked_ref,
):
    sources, samples = ranked_ref.shape[0], ranked_ref.shape[2]
    owners, pairs = raws_ref.shape[0], raws_ref.shape[1] // sources
    channels = pairs // local
    me = me_ref[0]
    wide[...] = raws_ref[...].astype(F32)
    chunks = samples // LANES
    member = iota((pairs, samples), 0) // channels

    def unslot(s, carry):
        name = name_ref[s, :pairs, :]
        at = pl.ds(pl.multiple_of(s * pairs, pairs), pairs)
        block = wide[:, at, :].reshape(owners * pairs, capacity).astype(BF16)
        pick = hot(iota((capacity, samples), 0) == rank_ref[s, :1, :])
        ranked_ref[s] = pick
        spread = dot(block, pick)
        total = jnp.zeros((pairs, samples), F32)
        for o in range(owners):
            total = total + jnp.where(name - o * local == member, spread[o * pairs : (o + 1) * pairs], 0.0)
        flat = total[:channels]
        for x in range(1, local):
            flat = flat + total[x * channels : (x + 1) * channels]
        for k in range(chunks):
            for c in range(channels):
                dense[c, pl.ds(s * chunks + k, 1), :] = flat[c : c + 1, k * LANES : (k + 1) * LANES]
        return carry

    lax.fori_loop(0, sources, unslot, 0, unroll=4)

    shades, graw = composite(
        [dense[c] for c in range(channels)],
        laid_ref[0],
        [laid_ref[c] for c in range(1, channels)],
        [laid_ref[c] for c in range(channels, 2 * channels - 1)],
    )
    for c in range(channels):
        grad[c] = graw[c]
    for c in range(channels - 1):
        dense[c] = shades[c]
        rendered_ref[c] = dense[c, pl.ds(pl.multiple_of(me * chunks, chunks), chunks), :]

    parts = [[] for _ in range(local)]
    for s in range(sources):
        own = name_ref[s, :pairs, :] - me * local == member
        flat = jnp.concatenate([lane_row(grad[c, s * chunks : (s + 1) * chunks, :]) for c in range(channels)], axis=0)
        high, low = split(jnp.where(own, jnp.concatenate([flat] * local, axis=0), 0.0))
        got = dot_nt(jnp.concatenate([high, low], axis=0), ranked_ref[s])
        for x in range(local):
            parts[x].append(
                jnp.concatenate(
                    [got[x * channels : (x + 1) * channels], got[pairs + x * channels : pairs + (x + 1) * channels]],
                    axis=0,
                )
            )
    head_total = None
    for x in range(local):
        part = jnp.concatenate(parts[x], axis=1).astype(BF16)
        gslot_ref[x] = part
        add = dot(part, act_ref[x])
        head_total = add if head_total is None else head_total + add
    head_total = head_total[:channels] + head_total[channels:]
    for d in range(headpart_ref.shape[0]):
        headpart_ref[d] = head_total


def backward_kernel(copies, me_ref, slope_in, actt_in, gslot_ref, enct_ref, hidden_ref, head_ref, *rest):
    outs, (gfirst, ghidden, slope_ref, actt_ref, moved) = rest[: 2 * copies], rest[2 * copies :]
    local = gslot_ref.shape[0]
    layers = hidden_ref.shape[1] + 1
    loads = []
    for layer in range(layers):
        some = [pltpu.make_async_copy(slope_in.at[layer], slope_ref.at[layer], moved.at[0, layer])]
        if layer:
            some.append(pltpu.make_async_copy(actt_in.at[layer - 1], actt_ref.at[layer - 1], moved.at[1, layer]))
        loads.append(some)
    for some in reversed(loads):
        for load in some:
            load.start()
    head = head_ref[...] * 0.5
    head = jnp.concatenate([head, head], axis=0)
    up = [dot_tn(gslot_ref[x], head).astype(BF16) for x in range(local)]
    for layer in reversed(range(layers)):
        for load in loads[layer]:
            load.wait()
        for x in range(local):
            glin = up[x] * slope_ref[layer, x]
            if layer:
                ghidden[x, layer - 1] = dot(actt_ref[layer - 1, x], glin)
                up[x] = dot_nt(glin, hidden_ref[x, layer - 1]).astype(BF16)
            else:
                gfirst[x] = dot(enct_ref[x], glin)
    me = me_ref[0]
    for s in range(copies):
        first_out, hidden_out = outs[2 * s], outs[2 * s + 1]
        piece = lax.rem(me + s, copies)
        size = first_out.shape[1]
        first_out[...] = gfirst[:, pl.ds(pl.multiple_of(piece * size, size), size), :]
        size = hidden_out.shape[2]
        hidden_out[...] = ghidden[:, :, pl.ds(pl.multiple_of(piece * size, size), size), :]


def head_kernel(heads_ref, out_ref):
    out_ref[...] = jnp.sum(heads_ref[...], axis=0)


def sum_kernel(copies, head_ref, *refs):
    pieces, outs, (first_ref, hidden_ref, done) = refs[: 2 * copies], refs[2 * copies : 2 * copies + 2], refs[2 * copies + 2 :]
    for k, held in enumerate((hidden_ref, first_ref)):
        total = pieces[1 - k][...]
        for s in range(1, copies):
            total = total + pieces[2 * s + 1 - k][...]
        held[...] = total
        pltpu.make_async_copy(held, outs[1 - k], done.at[k]).start()
    for k, held in enumerate((hidden_ref, first_ref)):
        pltpu.make_async_copy(held, outs[1 - k], done.at[k]).wait()


def shape(dims, dtype):
    return jax.ShapeDtypeStruct(dims, dtype)


def call(kernel, outs, ins, scratch=(), scalars=0, outside=(0, 0), flops=0, limit=24, pinned=True):
    specs = [pl.BlockSpec(memory_space=pltpu.SMEM)] * scalars
    specs += [pl.BlockSpec(memory_space=pl.ANY)] * outside[0]
    specs += [pl.BlockSpec(memory_space=VMEM)] * (len(ins) - len(specs))
    out_specs = [pl.BlockSpec(memory_space=pl.ANY)] * outside[1]
    out_specs += [pl.BlockSpec(memory_space=VMEM)] * (len(outs) - len(out_specs))
    held = [
        x if i < scalars else pltpu.with_memory_space_constraint(x, pltpu.HBM if i < scalars + outside[0] else VMEM)
        for i, x in enumerate(ins)
    ]
    return pl.pallas_call(
        kernel,
        out_shape=[
            (pltpu.HBM if i < outside[1] else VMEM)(x.shape, x.dtype) if pinned else x for i, x in enumerate(outs)
        ],
        in_specs=specs,
        out_specs=out_specs,
        scratch_shapes=list(scratch),
        cost_estimate=pl.CostEstimate(flops=flops, bytes_accessed=0, transcendentals=0),
        compiler_params=pltpu.CompilerParams(vmem_limit_bytes=limit * 1024 * 1024),
    )(*held)


def per_device(
    encoded, region_id, spacing, frame_index, target_rgb, frame_code, first_weight, hidden_weight, head_weight
):
    owners, copies = lax.axis_size("expert"), lax.axis_size("replica")
    local = first_weight.shape[0]
    experts = owners * local
    samples, enc_width = encoded.shape
    capacity = 2 * samples // experts
    hid = first_weight.shape[2]
    layers = hidden_weight.shape[1] + 1
    channels = head_weight.shape[0]
    chunks = samples // LANES
    slots = local * capacity
    rows = owners * capacity
    owner = lax.axis_index("expert").astype(jnp.int32).reshape(1)
    copy = lax.axis_index("replica").astype(jnp.int32).reshape(1)

    inputs = [
        region_id.reshape(chunks, LANES),
        encoded,
        spacing.reshape(chunks, LANES),
        frame_index.reshape(1, -1),
        target_rgb,
        frame_code,
        first_weight,
        hidden_weight,
        head_weight,
    ]
    outbound, first_half, hidden_half, head = call(
        functools.partial(dispatch_kernel, experts, capacity),
        [
            shape((owners, slots + META, enc_width), BF16),
            shape(first_weight.shape, BF16),
            shape(hidden_weight.shape, BF16),
            shape(head_weight.shape, BF16),
        ],
        inputs,
        [pltpu.VMEM(x.shape, x.dtype) for x in inputs]
        + [
            pltpu.VMEM((owners, slots + META, enc_width), BF16),
            pltpu.SemaphoreType.DMA((len(inputs),)),
            pltpu.SemaphoreType.DMA((owners,)),
        ],
        outside=(len(inputs), 1),
    )
    recv = lax.all_to_all(outbound, "expert", split_axis=0, concat_axis=0, tiled=True)
    pairs = local * channels
    big = (layers, local, rows, hid)
    tile = 2
    acts, slopes, raw, top = call(
        functools.partial(forward_kernel, capacity, tile),
        [
            shape((layers - 1, local, rows, hid), BF16),
            shape(big, BF16),
            shape((owners, owners * pairs, capacity), BF16),
            shape((local, rows, hid), BF16),
        ],
        [recv, first_half, hidden_half, head],
        [
            pltpu.VMEM((owners * pairs, capacity), F32),
            pltpu.VMEM((layers - 1, local, rows, hid), BF16),
            pltpu.VMEM(big, BF16),
            pltpu.SemaphoreType.DMA((2, owners // tile)),
        ],
        outside=(0, 2),
        flops=10**9,
    )
    raws = lax.all_to_all(raw, "expert", split_axis=0, concat_axis=0, tiled=True)
    flipped = (layers - 1, local, hid, rows)
    actt, order, names, laid, enct = call(
        functools.partial(plan_kernel, local, capacity),
        [
            shape(flipped, BF16),
            shape((owners, 8, samples), jnp.int32),
            shape((owners, 8, samples), jnp.int32),
            shape((2 * channels - 1, owners * chunks, LANES), F32),
            shape((local, enc_width, rows), BF16),
        ],
        [acts, recv],
        [
            pltpu.VMEM((layers - 1, local, rows, hid), BF16),
            pltpu.VMEM(flipped, BF16),
            pltpu.SemaphoreType.DMA((2, layers - 1)),
        ],
        outside=(1, 1),
        flops=5 * 10**9,
    )
    gslot, headpart, rendered = call(
        functools.partial(render_kernel, local, capacity),
        [
            shape((local, 2 * channels, rows), BF16),
            shape((owners * copies, channels, hid), F32),
            shape((channels - 1, chunks, LANES), F32),
        ],
        [owner, top, raws, order, names, laid],
        [
            pltpu.VMEM((owners, owners * pairs, capacity), F32),
            pltpu.VMEM((channels, owners * chunks, LANES), F32),
            pltpu.VMEM((channels, owners * chunks, LANES), F32),
            pltpu.VMEM((owners, capacity, samples), BF16),
        ],
        scalars=1,
        flops=10**9,
    )
    heads = lax.all_to_all(headpart, ("expert", "replica"), split_axis=0, concat_axis=0, tiled=True)
    pieces = []
    for _ in range(copies):
        pieces.append(shape((local, enc_width // copies, hid), F32))
        pieces.append(shape((local, layers - 1, hid // copies, hid), F32))
    grads = call(
        functools.partial(backward_kernel, copies),
        pieces,
        [copy, slopes, actt, gslot, enct, hidden_half, head],
        [
            pltpu.VMEM(first_weight.shape, F32),
            pltpu.VMEM(hidden_weight.shape, F32),
            pltpu.VMEM(big, BF16),
            pltpu.VMEM(flipped, BF16),
            pltpu.SemaphoreType.DMA((2, layers)),
        ],
        scalars=1,
        outside=(2, 0),
        flops=5 * 10**9,
    )
    grads = list(grads)
    for s in range(1, copies):
        ring = [(i, (i + s) % copies) for i in range(copies)]
        for k in (2 * s, 2 * s + 1):
            grads[k] = lax.ppermute(grads[k], "replica", ring)
    (head_grad,) = call(head_kernel, [shape((channels, hid), F32)], [heads], flops=10**11, pinned=False)
    first_grad, hidden_grad = call(
        functools.partial(sum_kernel, copies),
        [shape(grads[0].shape, F32), shape(grads[1].shape, F32)],
        [head_grad, *grads],
        [pltpu.VMEM(grads[0].shape, F32), pltpu.VMEM(grads[1].shape, F32), pltpu.SemaphoreType.DMA((2,))],
        outside=(1, 2),
    )
    rendered = rendered[:, :, ::RAY_SAMPLES].reshape(channels - 1, -1)
    return (first_grad, hidden_grad, head_grad, rendered)


def solution(mesh):
    placed = (
        P(("groups", "expert", "replica"), None),
        P(("groups", "expert", "replica")),
        P(("groups", "expert", "replica")),
        P(("groups", "expert", "replica")),
        P(None, ("groups", "expert", "replica")),
        P(None, "groups"),
        P("expert", None, None),
        P("expert", None, None, None),
        P(),
    )
    return jax.shard_map(
        per_device,
        mesh=mesh,
        in_specs=placed,
        out_specs=(
            P(("groups", "expert"), "replica", None),
            P(("groups", "expert"), None, "replica", None),
            P("groups", None),
            P(None, ("groups", "expert", "replica")),
        ),
        check_vma=False,
    )
```

time: 80.2 us -> 61.6 us (0.77)
  waiting for transfers between devices: 28.1 us -> 18.5 us
  local copies, waits for them, and re-layouts: 11.2 us -> 4.18 us
  other arithmetic: 2.27 us -> 0 us
    all_to_all x1, waiting for transfers between devices: 6.12 us -> 0.3 us  [per_device(): lax.all_to_all(headpart, ('expert', 'replica'), split_axis=0, concat_axis...]
    unnamed x26 -> x8, local copies, waits for them, and re-layouts: 9.14 us -> 3.44 us
    all_to_all x1, waiting for transfers between devices: 6.04 us -> 1.95 us  [per_device(): lax.all_to_all(raw, 'expert', split_axis=0, concat_axis=0, tiled=True)]
    add x2 -> x0, other arithmetic: 1.65 us -> none  [the longest x1 0.98 us: per_device(): hidden_grad = hidden_grad + lax.ppermute(grads[2 * s + 1], 'replica', ring)]
    squeeze x1 -> x0, local copies, waits for them, and re-layouts: 1.29 us -> none  [per_device(): acts[layers - 1]]
    pallas_call x4 -> x7, Pallas kernels: 22.4 us -> 22.1 us  [call(): pl.pallas_call(kernel, out_shape=[(pltpu.HBM if i < outside[1] else VMEM)...]
  transfers between devices with their start and end apart: 5 -> 5, of which waited for: 3 -> 4; matrix products, arithmetic and copies ran while one was open for 4% -> 1% of each run, Pallas kernels for 0% -> 14%
where the time goes in v2:
time: 61.6 us; the launch traced here: 61.1 us
  Pallas kernels  22.1 us (36%)
  waiting for transfers between devices  18.5 us (30%)
  starting transfers between devices  15.6 us (25%)
  local copies, waits for them, and re-layouts  4.18 us (7%)
  between operations  0.7 us (1%)
    pallas_call x7, Pallas kernels, call(): pl.pallas_call(kernel, out_shape=[(pltpu.HBM if i < outside[1] else VMEM)...  22.1 us
    all_to_all x1, waiting for transfers between devices, per_device(): lax.all_to_all(outbound, 'expert', split_axis=0, concat_axis=0, tiled=True)  15.9 us
    all_to_all x1, starting transfers between devices, per_device(): lax.all_to_all(outbound, 'expert', split_axis=0, concat_axis=0, tiled=True)  7.26 us
    all_to_all x1, starting transfers between devices, per_device(): lax.all_to_all(headpart, ('expert', 'replica'), split_axis=0, concat_axis...  4.16 us
    all_to_all x1, starting transfers between devices, per_device(): lax.all_to_all(raw, 'expert', split_axis=0, concat_axis=0, tiled=True)  3.65 us
    unnamed x8, local copies, waits for them, and re-layouts  3.44 us
    all_to_all x1, waiting for transfers between devices, per_device(): lax.all_to_all(raw, 'expert', split_axis=0, concat_axis=0, tiled=True)  1.95 us
  transfers between devices with their start and end apart: 5, of which 4 were waited for; matrix products, arithmetic and copies ran while one was open for 1% of the time, Pallas kernels for 14%

profile of v2, /device:TPU:0, one launch (start us, length us, event | category | flops | bytes accessed | tf_op | source)
XLA Modules:
  0.0 61.1 jit_solution(8290693778708146081)
XLA Ops:
  0.6 3.8 %shard_map.120 = (bf16[8,288,128]{2,1,0:T(8,128)(2,1)}, bf16[2,128,256]{2,1,0:T(8,128)(2,1)S(1)}, bf16[2,3,256,256]{3,2,1,0:T(8,128)(2,1)S(1)}, bf16[4,256]{1,0:T(4,128)(2,1)S(1)}) custom-call(s32[8,128]{1,0:T(8,128)} %bitcast.5, bf16[1024,128]{1,0:T(8,128)(2,1)} %refs_1_.1, f32[8,128]{1,0:T(8,128)} %bitcast.6, s32[1,16]{1,0:T(1,128)} %bitcast.7, ...), custom_call_target="tpu_custom_call" | custom-call | tf_op jit(solution)/shard_map/pallas_call | solution.py:401
  4.4 7.3 %all-to-all-start = ((bf16[8,288,128]{2,1,0:T(8,128)(2,1)}), bf16[8,288,128]{2,1,0:T(8,128)(2,1)S(1)}, u32[]{:S(2)}, u32[]{:S(2)}) async-start(bf16[8,288,128]{2,1,0:T(8,128)(2,1)} %get-tuple-element.26), calls=%async_computation | async-start | bytes 1179648 | tf_op jit(solution)/shard_map/all_to_all | solution.py:459
  11.7 15.9 %all-to-all-done.recv_ref = bf16[8,288,128]{2,1,0:T(8,128)(2,1)S(1)} async-done(((bf16[8,288,128]{2,1,0:T(8,128)(2,1)}), bf16[8,288,128]{2,1,0:T(8,128)(2,1)S(1)}, u32[]{:S(2)}, u32[]{:S(2)}) %all-to-all-start) | async-done | bytes 589856 | tf_op jit(solution)/shard_map/all_to_all | solution.py:459
  27.6 5.6 %shard_map.121 = (bf16[3,2,1024,256]{3,2,1,0:T(8,128)(2,1)}, bf16[4,2,1024,256]{3,2,1,0:T(8,128)(2,1)}, bf16[8,64,128]{2,1,0:T(8,128)(2,1)}, bf16[2,1024,256]{2,1,0:T(8,128)(2,1)S(1)}) custom-call(bf16[8,288,128]{2,1,0:T(8,128)(2,1)S(1)} %all-to-all-done.recv_ref, bf16[2,128,256]{2,1,0:T(8,128)(2,1)S(1)} %get-tuple-element.27.first_ref, ...), custom_call_target="tpu_custom_call" | custom-call | flops 1000000000 | tf_op jit(solution)/shard_map/pallas_call | solution.py:401
  33.1 3.7 %all-to-all-start.1 = ((bf16[8,64,128]{2,1,0:T(8,128)(2,1)}), bf16[8,64,128]{2,1,0:T(8,128)(2,1)S(1)}, u32[]{:S(2)}, u32[]{:S(2)}) async-start(bf16[8,64,128]{2,1,0:T(8,128)(2,1)} %get-tuple-element.31), calls=%async_computation.1 | async-start | bytes 262144 | tf_op jit(solution)/shard_map/all_to_all | solution.py:481
  36.8 3.9 %shard_map.122 = (bf16[3,2,256,1024]{3,2,1,0:T(8,128)(2,1)}, s32[8,8,1024]{2,1,0:T(8,128)S(1)}, s32[8,8,1024]{2,1,0:T(8,128)S(1)}, f32[7,64,128]{2,1,0:T(8,128)S(1)}, bf16[2,128,1024]{2,1,0:T(8,128)(2,1)S(1)}) custom-call(bf16[3,2,1024,256]{3,2,1,0:T(8,128)(2,1)} %get-tuple-element.32.act_in, bf16[8,288,128]{2,1,0:T(8,128)(2,1)S(1)} %all-to-all-done.recv_ref), custom_call_target="tpu_custom_call" | custom-call | flops 5000000000 | tf_op jit(solution)/shard_map/pallas_call | solution.py:401
  40.7 0.0 copy-start
  40.7 0.7 %copy-done = f32[7,64,128]{2,1,0:T(8,128)} copy-done((f32[7,64,128]{2,1,0:T(8,128)}, f32[7,64,128]{2,1,0:T(8,128)S(1)}, u32[]{:S(2)}) %copy-start) | copy-done | bytes 229400
  41.4 0.0 copy-start.2
  41.4 0.8 %copy-done.2 = bf16[2,128,1024]{2,1,0:T(8,128)(2,1)} copy-done((bf16[2,128,1024]{2,1,0:T(8,128)(2,1)}, bf16[2,128,1024]{2,1,0:T(8,128)(2,1)S(1)}, u32[]{:S(2)}) %copy-start.2) | copy-done | bytes 524312
  42.2 1.9 %all-to-all-done.1.raws_ref = bf16[8,64,128]{2,1,0:T(8,128)(2,1)S(1)} async-done(((bf16[8,64,128]{2,1,0:T(8,128)(2,1)}), bf16[8,64,128]{2,1,0:T(8,128)(2,1)S(1)}, u32[]{:S(2)}, u32[]{:S(2)}) %all-to-all-start.1) | async-done | bytes 131104 | tf_op jit(solution)/shard_map/all_to_all | solution.py:481
  44.1 0.0 copy-start.1
  44.1 0.9 %copy-done.1 = f32[7,64,128]{2,1,0:T(8,128)S(1)} copy-done((f32[7,64,128]{2,1,0:T(8,128)S(1)}, f32[7,64,128]{2,1,0:T(8,128)}, u32[]{:S(2)}) %copy-start.1) | copy-done | bytes 229400
  45.1 3.0 %shard_map.123 = (bf16[2,8,1024]{2,1,0:T(8,128)(2,1)S(1)}, f32[16,4,256]{2,1,0:T(4,128)}, f32[3,8,128]{2,1,0:T(8,128)S(1)}) custom-call(s32[1]{0:T(128)} %bitcast.me_ref, bf16[2,1024,256]{2,1,0:T(8,128)(2,1)S(1)} %get-tuple-element.30.act_ref, bf16[8,64,128]{2,1,0:T(8,128)(2,1)S(1)} %all-to-all-done.1.raws_ref, ...), custom_call_target="tpu_custom_call" | custom-call | flops 1000000000 | tf_op jit(solution)/shard_map/pallas_call | solution.py:401
  48.1 4.2 %all-to-all-start.2 = ((f32[16,4,256]{2,1,0:T(4,128)}), f32[16,4,256]{2,1,0:T(4,128)S(1)}, u32[]{:S(2)}, u32[]{:S(2)}) async-start(f32[16,4,256]{2,1,0:T(4,128)} %get-tuple-element.36), calls=%async_computation.2 | async-start | bytes 131072 | tf_op jit(solution)/shard_map/all_to_all | solution.py:518
  52.3 0.0 copy-start.3
  52.3 1.0 %copy-done.3 = bf16[2,128,1024]{2,1,0:T(8,128)(2,1)S(1)} copy-done((bf16[2,128,1024]{2,1,0:T(8,128)(2,1)S(1)}, bf16[2,128,1024]{2,1,0:T(8,128)(2,1)}, u32[]{:S(2)}) %copy-start.3) | copy-done | bytes 524312
  53.3 4.2 %shard_map.125 = (f32[2,64,256]{2,1,0:T(8,128)S(1)}, f32[2,3,128,256]{3,2,1,0:T(8,128)S(1)}, f32[2,64,256]{2,1,0:T(8,128)S(1)}, f32[2,3,128,256]{3,2,1,0:T(8,128)S(1)}) custom-call(s32[1]{0:T(128)} %bitcast.4.me_ref, bf16[4,2,1024,256]{3,2,1,0:T(8,128)(2,1)} %get-tuple-element.37.slope_in, bf16[3,2,256,1024]{3,2,1,0:T(8,128)(2,1)} %get-tuple-element.38.actt_in, ...), custom_call_target="tpu_custom_call" | custom-call | flops 5000000000 | tf_op jit(solution)/shard_map/pallas_call | solution.py:401
  57.5 0.5 collective-permute-start.1
  58.0 0.1 collective-permute-start
  58.1 0.1 slice.3
  58.2 0.7 %reshape.31 = f32[3,16]{1,0:T(4,128)} reshape(f32[3,8,2]{2,1,0:T(8,128)S(1)} %slice.3) | data formatting | bytes 384 | tf_op jit(solution)/shard_map/reshape | solution.py:551
  58.9 0.3 all-to-all-done.2.heads_ref
  59.2 0.6 %shard_map.124.head_ref = f32[4,256]{1,0:T(4,128)} custom-call(f32[16,4,256]{2,1,0:T(4,128)S(1)} %all-to-all-done.2.heads_ref), custom_call_target="tpu_custom_call" | custom-call | flops 99999997952 | tf_op jit(solution)/shard_map/pallas_call | solution.py:401
  59.8 0.3 collective-permute-done.refs_2_
  60.1 0.0 collective-permute-done.1.refs_3_
  60.1 1.0 %shard_map.126 = (f32[2,64,256]{2,1,0:T(8,128)}, f32[2,3,128,256]{3,2,1,0:T(8,128)}) custom-call(f32[4,256]{1,0:T(4,128)} %shard_map.124.head_ref, f32[2,64,256]{2,1,0:T(8,128)S(1)} %get-tuple-element.41.refs_0_, f32[2,3,128,256]{3,2,1,0:T(8,128)S(1)} %get-tuple-element.42.refs_1_, f32[2,64,256]{2,1,0:T(8,128)S(1)} %collective-permute-done.refs_2_, ...), custom_call_target="tpu_custom_call" | custom-call | tf_op jit(solution)/shard_map/pallas_call | solution.py:401
Async XLA Ops:
  4.4 23.2 %all-to-all-start = ((bf16[8,288,128]{2,1,0:T(8,128)(2,1)}), bf16[8,288,128]{2,1,0:T(8,128)(2,1)S(1)}, u32[]{:S(2)}, u32[]{:S(2)}) async-start(bf16[8,288,128]{2,1,0:T(8,128)(2,1)} %get-tuple-element.26), calls=%async_computation | async-start | bytes 1179648 | tf_op jit(solution)/shard_map/all_to_all | solution.py:459
  33.1 11.0 %all-to-all-start.1 = ((bf16[8,64,128]{2,1,0:T(8,128)(2,1)}), bf16[8,64,128]{2,1,0:T(8,128)(2,1)S(1)}, u32[]{:S(2)}, u32[]{:S(2)}) async-start(bf16[8,64,128]{2,1,0:T(8,128)(2,1)} %get-tuple-element.31), calls=%async_computation.1 | async-start | bytes 262144 | tf_op jit(solution)/shard_map/all_to_all | solution.py:481
  40.7 0.7 %copy-start = (f32[7,64,128]{2,1,0:T(8,128)}, f32[7,64,128]{2,1,0:T(8,128)S(1)}, u32[]{:S(2)}) copy-start(f32[7,64,128]{2,1,0:T(8,128)S(1)} %get-tuple-element.35.laid_ref) | copy-start | bytes 688132
  41.4 0.8 %copy-start.2 = (bf16[2,128,1024]{2,1,0:T(8,128)(2,1)}, bf16[2,128,1024]{2,1,0:T(8,128)(2,1)S(1)}, u32[]{:S(2)}) copy-start(bf16[2,128,1024]{2,1,0:T(8,128)(2,1)S(1)} %get-tuple-element.40.enct_ref) | copy-start | bytes 1572868
  44.1 0.9 %copy-start.1 = (f32[7,64,128]{2,1,0:T(8,128)S(1)}, f32[7,64,128]{2,1,0:T(8,128)}, u32[]{:S(2)}) copy-start(f32[7,64,128]{2,1,0:T(8,128)} %copy-done) | copy-start | bytes 688132
  48.1 11.1 %all-to-all-start.2 = ((f32[16,4,256]{2,1,0:T(4,128)}), f32[16,4,256]{2,1,0:T(4,128)S(1)}, u32[]{:S(2)}, u32[]{:S(2)}) async-start(f32[16,4,256]{2,1,0:T(4,128)} %get-tuple-element.36), calls=%async_computation.2 | async-start | bytes 131072 | tf_op jit(solution)/shard_map/all_to_all | solution.py:518
  52.3 1.0 %copy-start.3 = (bf16[2,128,1024]{2,1,0:T(8,128)(2,1)S(1)}, bf16[2,128,1024]{2,1,0:T(8,128)(2,1)}, u32[]{:S(2)}) copy-start(bf16[2,128,1024]{2,1,0:T(8,128)(2,1)} %copy-done.2) | copy-start | bytes 1572868
  57.5 2.6 %collective-permute-start.1 = (f32[2,3,128,256]{3,2,1,0:T(8,128)S(1)}, f32[2,3,128,256]{3,2,1,0:T(8,128)S(1)}, u32[]{:S(2)}, u32[]{:S(2)}) collective-permute-start(f32[2,3,128,256]{3,2,1,0:T(8,128)S(1)} %get-tuple-element.44), channel_id=1, source_target_pairs={{0,1},{1,0},{2,3},{3,2},{4,5},{5,4},{6,7},{7,6},{8,9},{9,8},{10,11... | collective-permute-start | bytes 2359304 | tf_op jit(solution)/shard_map/ppermute | solution.py:542
  58.0 2.1 %collective-permute-start = (f32[2,64,256]{2,1,0:T(8,128)S(1)}, f32[2,64,256]{2,1,0:T(8,128)S(1)}, u32[]{:S(2)}, u32[]{:S(2)}) collective-permute-start(f32[2,64,256]{2,1,0:T(8,128)S(1)} %get-tuple-element.43), channel_id=1, source_target_pairs={{0,1},{1,0},{2,3},{3,2},{4,5},{5,4},{6,7},{7,6},{8,9},{9,8},{10,11... | collective-permute-start | bytes 393224 | tf_op jit(solution)/shard_map/ppermute | solution.py:542

commit v3 on v2

--- a/solution.py
+++ b/solution.py
@@ -60,15 +60,14 @@
 
 
 def dispatch_kernel(experts, capacity, *refs):
-    outside, (out_ref, first_out, hidden_out, head_out), refs = refs[:9], refs[9:13], refs[13:]
-    inside, (held, loaded, sent) = refs[:9], refs[9:]
+    outside, out_ref, inside, (held, loaded, sent) = refs[:6], refs[6], refs[7:13], refs[13:]
     loads = [pltpu.make_async_copy(a, b, loaded.at[i]) for i, (a, b) in enumerate(zip(outside, inside))]
     for load in loads:
         load.start()
-    region_ref, enc_ref, spacing_ref, frame_ref, target_ref, code_ref, first_ref, hidden_ref, head_ref = inside
+    region_ref, enc_ref, spacing_ref, frame_ref, target_ref, code_ref = inside
     owners, rows = held.shape[0], held.shape[1] - META
     samples = enc_ref.shape[0]
-    for load in loads[:6]:
+    for load in loads:
         load.wait()
     region = region_ref[...]
     slot = lane_row(region * capacity + ranks(region, experts))
@@ -100,18 +99,27 @@
         send(d).start()
         return carry
 
-    lax.fori_loop(0, owners, one, 0, unroll=2)
-    for load in loads[6:]:
+    lax.fori_loop(0, owners, one, 0, unroll=8)
+
+    def finish(d, carry):
+        send(d).wait()
+        return carry
+
+    lax.fori_loop(0, owners, finish, 0)
+
+
+def weight_kernel(first_in, hidden_in, head_in, first_out, hidden_out, head_out, first_ref, hidden_ref, moved):
+    loads = [
+        pltpu.make_async_copy(first_in, first_ref, moved.at[0]),
+        pltpu.make_async_copy(hidden_in, hidden_ref, moved.at[1]),
+        pltpu.make_async_copy(head_in, head_out, moved.at[2]),
+    ]
+    for load in loads:
+        load.start()
+    for load in loads:
         load.wait()
     first_out[...] = first_ref[...] * 0.5
     hidden_out[...] = hidden_ref[...] * 0.5
-    head_out[...] = head_ref[...]
-
-    def finish(d, carry):
-        send(d).wait()
-        return carry
-
-    lax.fori_loop(0, owners, finish, 0)
 
 
 def layer_forward(half):
@@ -121,7 +129,20 @@
 
 
 def forward_kernel(
-    capacity, tile, recv_ref, first_ref, hidden_ref, head_ref, act_out, slope_out, raw_ref, top_ref, held, act_ref, slope_ref, done
+    capacity,
+    tile,
+    recv_ref,
+    first_ref,
+    hidden_ref,
+    head_ref,
+    act_out,
+    slope_out,
+    raw_ref,
+    act_top,
+    held,
+    act_ref,
+    slope_ref,
+    done,
 ):
     sources = recv_ref.shape[0]
     local = first_ref.shape[0]
@@ -129,35 +150,39 @@
     head = head_ref[...]
     pairs = local * head.shape[0]
 
-    def saves(t):
-        at = pl.ds(pl.multiple_of(t * tile * capacity, tile * capacity), tile * capacity)
-        return (
-            pltpu.make_async_copy(act_ref.at[:, :, at, :], act_out.at[:, :, at, :], done.at[0, t]),
-            pltpu.make_async_copy(slope_ref.at[:, :, at, :], slope_out.at[:, :, at, :], done.at[1, t]),
-        )
+    def rows_of(t):
+        return pl.ds(pl.multiple_of(t * tile * capacity, tile * capacity), tile * capacity)
+
+    def saves(t, layer):
+        at = rows_of(t)
+        pairs_of = [(slope_ref, slope_out)] + ([(act_ref, act_out)] if layer < layers - 1 else [])
+        return [
+            pltpu.make_async_copy(a.at[layer, :, at, :], b.at[layer, :, at, :], done.at[k, layer, t])
+            for k, (a, b) in enumerate(pairs_of)
+        ]
 
     def step(t, carry):
         current = []
         for x in range(local):
             block = recv_ref[pl.ds(t * tile, tile), x * capacity : (x + 1) * capacity, :]
             current.append(block.reshape(tile * capacity, block.shape[2]))
-        at = pl.ds(pl.multiple_of(t * tile * capacity, tile * capacity), tile * capacity)
+        at = rows_of(t)
         for layer in range(layers):
             for x in range(local):
                 weight = first_ref[x] if layer == 0 else hidden_ref[x, layer - 1]
                 act, slope = layer_forward(dot(current[x], weight))
+                slope_ref[layer, x, at, :] = slope
                 if layer < layers - 1:
                     act_ref[layer, x, at, :] = act
                 else:
-                    top_ref[x, at, :] = act
-                slope_ref[layer, x, at, :] = slope
+                    act_top[x, at, :] = act
                 current[x] = act
+            for save in saves(t, layer):
+                save.start()
         raws = [dot_nt(head, current[x]) for x in range(local)]
         for s in range(tile):
             both = jnp.concatenate([r[:, s * capacity : (s + 1) * capacity] for r in raws], axis=0)
             held[pl.ds(pl.multiple_of((t * tile + s) * pairs, pairs), pairs), :] = both
-        for save in saves(t):
-            save.start()
         return carry
 
     lax.fori_loop(0, sources // tile, step, 0)
@@ -166,8 +191,9 @@
         raw_ref[d] = raw
 
     def finish(t, carry):
-        for save in saves(t):
-            save.wait()
+        for layer in range(layers):
+            for save in saves(t, layer):
+                save.wait()
         return carry
 
     lax.fori_loop(0, sources // tile, finish, 0)
@@ -207,7 +233,7 @@
 
 
 def plan_kernel(
-    local, capacity, act_in, recv_ref, actt_out, rank_ref, name_ref, laid_ref, enct_ref, act_ref, actt_ref, moved
+    local, capacity, act_in, recv_ref, actt_out, enct_out, rank_ref, name_ref, laid_ref, act_ref, actt_ref, enct_ref, moved
 ):
     layers = actt_ref.shape[0]
     loads = [pltpu.make_async_copy(act_in.at[k], act_ref.at[k], moved.at[0, k]) for k in range(layers)]
@@ -217,13 +243,13 @@
     sources, slots = recv_ref.shape[0], recv_ref.shape[1] - META
     rows = sources * capacity
     experts = sources * local
-    samples = rank_ref.shape[2]
+    samples = rank_ref.shape[1]
     chunks = samples // LANES
 
     def one(s, carry):
         region = recv_ref[s, slots : slots + chunks, :].astype(F32).astype(jnp.int32)
-        rank_ref[s] = jnp.broadcast_to(lane_row(ranks(region, experts)), (8, samples))
-        name_ref[s] = jnp.broadcast_to(lane_row(region), (8, samples))
+        rank_ref[pl.ds(s, 1), :] = lane_row(ranks(region, experts))
+        name_ref[pl.ds(s, 1), :] = lane_row(region)
         return carry
 
     lax.fori_loop(0, sources, one, 0, unroll=2)
@@ -242,6 +268,9 @@
 
     for x in range(local):
         enct_ref[x] = recv_ref[:, x * capacity : (x + 1) * capacity, :].reshape(rows, recv_ref.shape[2]).T
+    save = pltpu.make_async_copy(enct_ref, enct_out, moved.at[0, layers])
+    save.start()
+    saves.append(save)
     for layer in reversed(range(layers)):
         loads[layer].wait()
         for x in range(local):
@@ -255,20 +284,23 @@
     local,
     capacity,
     me_ref,
-    act_ref,
     raws_ref,
     rank_ref,
     name_ref,
     laid_ref,
+    act_ref,
+    rendered_out,
     gslot_ref,
     headpart_ref,
-    rendered_ref,
     wide,
     dense,
     grad,
     ranked_ref,
+    rendered_ref,
+    moved,
 ):
-    sources, samples = ranked_ref.shape[0], ranked_ref.shape[2]
+    save = pltpu.make_async_copy(rendered_ref, rendered_out, moved)
+    sources, samples = rank_ref.shape
     owners, pairs = raws_ref.shape[0], raws_ref.shape[1] // sources
     channels = pairs // local
     me = me_ref[0]
@@ -277,10 +309,10 @@
     member = iota((pairs, samples), 0) // channels
 
     def unslot(s, carry):
-        name = name_ref[s, :pairs, :]
+        name = name_ref[pl.ds(s, 1), :]
         at = pl.ds(pl.multiple_of(s * pairs, pairs), pairs)
         block = wide[:, at, :].reshape(owners * pairs, capacity).astype(BF16)
-        pick = hot(iota((capacity, samples), 0) == rank_ref[s, :1, :])
+        pick = hot(iota((capacity, samples), 0) == rank_ref[pl.ds(s, 1), :])
         ranked_ref[s] = pick
         spread = dot(block, pick)
         total = jnp.zeros((pairs, samples), F32)
@@ -304,13 +336,20 @@
     )
     for c in range(channels):
         grad[c] = graw[c]
+    rays = samples // RAY_SAMPLES
+    per_row = LANES // RAY_SAMPLES
+    pick = hot(iota((LANES, rays), 0) == iota((LANES, rays), 1) % per_row * RAY_SAMPLES, F32)
+    keep = iota((chunks, rays), 1) // per_row == iota((chunks, rays), 0)
     for c in range(channels - 1):
         dense[c] = shades[c]
-        rendered_ref[c] = dense[c, pl.ds(pl.multiple_of(me * chunks, chunks), chunks), :]
+        mine = dense[c, pl.ds(pl.multiple_of(me * chunks, chunks), chunks), :]
+        mine = jnp.dot(mine, pick, precision=lax.Precision.HIGHEST, preferred_element_type=F32)
+        rendered_ref[c : c + 1, :] = jnp.sum(jnp.where(keep, mine, 0.0), axis=0, keepdims=True)
+    save.start()
 
     parts = [[] for _ in range(local)]
     for s in range(sources):
-        own = name_ref[s, :pairs, :] - me * local == member
+        own = name_ref[s : s + 1, :] - me * local == member
         flat = jnp.concatenate([lane_row(grad[c, s * chunks : (s + 1) * chunks, :]) for c in range(channels)], axis=0)
         high, low = split(jnp.where(own, jnp.concatenate([flat] * local, axis=0), 0.0))
         got = dot_nt(jnp.concatenate([high, low], axis=0), ranked_ref[s])
@@ -330,34 +369,37 @@
     head_total = head_total[:channels] + head_total[channels:]
     for d in range(headpart_ref.shape[0]):
         headpart_ref[d] = head_total
-
-
-def backward_kernel(copies, me_ref, slope_in, actt_in, gslot_ref, enct_ref, hidden_ref, head_ref, *rest):
-    outs, (gfirst, ghidden, slope_ref, actt_ref, moved) = rest[: 2 * copies], rest[2 * copies :]
+    save.wait()
+
+
+def backward_kernel(copies, me_ref, slope_in, actt_in, enct_in, hidden_in, gslot_ref, head_ref, *rest):
+    outs, (gfirst, ghidden, slope_ref, actt_ref, enct_ref, hidden_ref, moved) = rest[: 2 * copies], rest[2 * copies :]
     local = gslot_ref.shape[0]
     layers = hidden_ref.shape[1] + 1
-    loads = []
-    for layer in range(layers):
-        some = [pltpu.make_async_copy(slope_in.at[layer], slope_ref.at[layer], moved.at[0, layer])]
-        if layer:
-            some.append(pltpu.make_async_copy(actt_in.at[layer - 1], actt_ref.at[layer - 1], moved.at[1, layer]))
-        loads.append(some)
-    for some in reversed(loads):
-        for load in some:
-            load.start()
+    fetch = [(slope_in.at[layers - 1], slope_ref.at[layers - 1]), (hidden_in, hidden_ref)]
+    for layer in reversed(range(layers - 1)):
+        fetch.append((slope_in.at[layer], slope_ref.at[layer]))
+        fetch.append((actt_in.at[layer], actt_ref.at[layer]))
+    fetch.append((enct_in, enct_ref))
+    loads = [pltpu.make_async_copy(a, b, moved.at[i]) for i, (a, b) in enumerate(fetch)]
+    for load in loads:
+        load.start()
     head = head_ref[...] * 0.5
     head = jnp.concatenate([head, head], axis=0)
     up = [dot_tn(gslot_ref[x], head).astype(BF16) for x in range(local)]
-    for layer in reversed(range(layers)):
-        for load in loads[layer]:
-            load.wait()
+    loads.pop(0).wait()
+    glin = [up[x] * slope_ref[layers - 1, x] for x in range(local)]
+    loads.pop(0).wait()
+    for layer in reversed(range(1, layers)):
+        up = [dot_nt(glin[x], hidden_ref[x, layer - 1] * 0.5).astype(BF16) for x in range(local)]
+        loads.pop(0).wait()
+        loads.pop(0).wait()
         for x in range(local):
-            glin = up[x] * slope_ref[layer, x]
-            if layer:
-                ghidden[x, layer - 1] = dot(actt_ref[layer - 1, x], glin)
-                up[x] = dot_nt(glin, hidden_ref[x, layer - 1]).astype(BF16)
-            else:
-                gfirst[x] = dot(enct_ref[x], glin)
+            ghidden[x, layer - 1] = dot(actt_ref[layer - 1, x], glin[x])
+            glin[x] = up[x] * slope_ref[layer - 1, x]
+    loads.pop(0).wait()
+    for x in range(local):
+        gfirst[x] = dot(enct_ref[x], glin[x])
     me = me_ref[0]
     for s in range(copies):
         first_out, hidden_out = outs[2 * s], outs[2 * s + 1]
@@ -373,7 +415,8 @@
 
 
 def sum_kernel(copies, head_ref, *refs):
-    pieces, outs, (first_ref, hidden_ref, done) = refs[: 2 * copies], refs[2 * copies : 2 * copies + 2], refs[2 * copies + 2 :]
+    pieces, outs, (first_ref, hidden_ref, done) = refs[: 2 * copies], refs[2 * copies : 2 * copies + 3], refs[2 * copies + 3 :]
+    pltpu.make_async_copy(head_ref, outs[2], done.at[2]).start()
     for k, held in enumerate((hidden_ref, first_ref)):
         total = pieces[1 - k][...]
         for s in range(1, copies):
@@ -382,13 +425,14 @@
         pltpu.make_async_copy(held, outs[1 - k], done.at[k]).start()
     for k, held in enumerate((hidden_ref, first_ref)):
         pltpu.make_async_copy(held, outs[1 - k], done.at[k]).wait()
+    pltpu.make_async_copy(head_ref, outs[2], done.at[2]).wait()
 
 
 def shape(dims, dtype):
     return jax.ShapeDtypeStruct(dims, dtype)
 
 
-def call(kernel, outs, ins, scratch=(), scalars=0, outside=(0, 0), flops=0, limit=24, pinned=True):
+def call(kernel, outs, ins, scratch=(), scalars=0, outside=(0, 0), flops=0, limit=24):
     specs = [pl.BlockSpec(memory_space=pltpu.SMEM)] * scalars
     specs += [pl.BlockSpec(memory_space=pl.ANY)] * outside[0]
     specs += [pl.BlockSpec(memory_space=VMEM)] * (len(ins) - len(specs))
@@ -401,7 +445,7 @@
     return pl.pallas_call(
         kernel,
         out_shape=[
-            (pltpu.HBM if i < outside[1] else VMEM)(x.shape, x.dtype) if pinned else x for i, x in enumerate(outs)
+            (pltpu.HBM if i < outside[1] else VMEM)(x.shape, x.dtype) for i, x in enumerate(outs)
         ],
         in_specs=specs,
         out_specs=out_specs,
@@ -435,18 +479,10 @@
         frame_index.reshape(1, -1),
         target_rgb,
         frame_code,
-        first_weight,
-        hidden_weight,
-        head_weight,
     ]
-    outbound, first_half, hidden_half, head = call(
+    (outbound,) = call(
         functools.partial(dispatch_kernel, experts, capacity),
-        [
-            shape((owners, slots + META, enc_width), BF16),
-            shape(first_weight.shape, BF16),
-            shape(hidden_weight.shape, BF16),
-            shape(head_weight.shape, BF16),
-        ],
+        [shape((owners, slots + META, enc_width), BF16)],
         inputs,
         [pltpu.VMEM(x.shape, x.dtype) for x in inputs]
         + [
@@ -456,63 +492,80 @@
         ],
         outside=(len(inputs), 1),
     )
+    first_half, hidden_half, head = call(
+        weight_kernel,
+        [shape(first_weight.shape, BF16), shape(hidden_weight.shape, BF16), shape(head_weight.shape, BF16)],
+        [first_weight, hidden_weight, head_weight],
+        [
+            pltpu.VMEM(first_weight.shape, BF16),
+            pltpu.VMEM(hidden_weight.shape, BF16),
+            pltpu.SemaphoreType.DMA((3,)),
+        ],
+        outside=(3, 0),
+        flops=3 * 10**9,
+    )
     recv = lax.all_to_all(outbound, "expert", split_axis=0, concat_axis=0, tiled=True)
     pairs = local * channels
-    big = (layers, local, rows, hid)
-    tile = 2
-    acts, slopes, raw, top = call(
+    tile = 4
+    top = (local, rows, hid)
+    lower = (layers - 1,) + top
+    acts, slopes, raw, act_top = call(
         functools.partial(forward_kernel, capacity, tile),
         [
-            shape((layers - 1, local, rows, hid), BF16),
-            shape(big, BF16),
+            shape(lower, BF16),
+            shape((layers,) + top, BF16),
             shape((owners, owners * pairs, capacity), BF16),
-            shape((local, rows, hid), BF16),
+            shape(top, BF16),
         ],
         [recv, first_half, hidden_half, head],
         [
             pltpu.VMEM((owners * pairs, capacity), F32),
-            pltpu.VMEM((layers - 1, local, rows, hid), BF16),
-            pltpu.VMEM(big, BF16),
-            pltpu.SemaphoreType.DMA((2, owners // tile)),
+            pltpu.VMEM(lower, BF16),
+            pltpu.VMEM((layers,) + top, BF16),
+            pltpu.SemaphoreType.DMA((2, layers, owners // tile)),
         ],
         outside=(0, 2),
         flops=10**9,
     )
     raws = lax.all_to_all(raw, "expert", split_axis=0, concat_axis=0, tiled=True)
     flipped = (layers - 1, local, hid, rows)
-    actt, order, names, laid, enct = call(
+    actt, enct, order, names, laid = call(
         functools.partial(plan_kernel, local, capacity),
         [
             shape(flipped, BF16),
-            shape((owners, 8, samples), jnp.int32),
-            shape((owners, 8, samples), jnp.int32),
+            shape((local, enc_width, rows), BF16),
+            shape((owners, samples), jnp.int32),
+            shape((owners, samples), jnp.int32),
             shape((2 * channels - 1, owners * chunks, LANES), F32),
-            shape((local, enc_width, rows), BF16),
         ],
         [acts, recv],
         [
-            pltpu.VMEM((layers - 1, local, rows, hid), BF16),
+            pltpu.VMEM(lower, BF16),
             pltpu.VMEM(flipped, BF16),
-            pltpu.SemaphoreType.DMA((2, layers - 1)),
-        ],
-        outside=(1, 1),
+            pltpu.VMEM((local, enc_width, rows), BF16),
+            pltpu.SemaphoreType.DMA((2, layers)),
+        ],
+        outside=(1, 2),
         flops=5 * 10**9,
     )
-    gslot, headpart, rendered = call(
+    rendered, gslot, headpart = call(
         functools.partial(render_kernel, local, capacity),
         [
+            shape(target_rgb.shape, F32),
             shape((local, 2 * channels, rows), BF16),
             shape((owners * copies, channels, hid), F32),
-            shape((channels - 1, chunks, LANES), F32),
-        ],
-        [owner, top, raws, order, names, laid],
+        ],
+        [owner, raws, order, names, laid, act_top],
         [
             pltpu.VMEM((owners, owners * pairs, capacity), F32),
             pltpu.VMEM((channels, owners * chunks, LANES), F32),
             pltpu.VMEM((channels, owners * chunks, LANES), F32),
             pltpu.VMEM((owners, capacity, samples), BF16),
+            pltpu.VMEM(target_rgb.shape, F32),
+            pltpu.SemaphoreType.DMA,
         ],
         scalars=1,
+        outside=(0, 1),
         flops=10**9,
     )
     heads = lax.all_to_all(headpart, ("expert", "replica"), split_axis=0, concat_axis=0, tiled=True)
@@ -523,16 +576,18 @@
     grads = call(
         functools.partial(backward_kernel, copies),
         pieces,
-        [copy, slopes, actt, gslot, enct, hidden_half, head],
+        [copy, slopes, actt, enct, hidden_weight, gslot, head],
         [
             pltpu.VMEM(first_weight.shape, F32),
             pltpu.VMEM(hidden_weight.shape, F32),
-            pltpu.VMEM(big, BF16),
+            pltpu.VMEM((layers,) + top, BF16),
             pltpu.VMEM(flipped, BF16),
-            pltpu.SemaphoreType.DMA((2, layers)),
+            pltpu.VMEM((local, enc_width, rows), BF16),
+            pltpu.VMEM(hidden_weight.shape, BF16),
+            pltpu.SemaphoreType.DMA((2 * layers + 1,)),
         ],
         scalars=1,
-        outside=(2, 0),
+        outside=(4, 0),
         flops=5 * 10**9,
     )
     grads = list(grads)
@@ -540,15 +595,14 @@
         ring = [(i, (i + s) % copies) for i in range(copies)]
         for k in (2 * s, 2 * s + 1):
             grads[k] = lax.ppermute(grads[k], "replica", ring)
-    (head_grad,) = call(head_kernel, [shape((channels, hid), F32)], [heads], flops=10**11, pinned=False)
-    first_grad, hidden_grad = call(
+    (head_grad,) = call(head_kernel, [shape((channels, hid), F32)], [heads], flops=10**11)
+    first_grad, hidden_grad, head_grad = call(
         functools.partial(sum_kernel, copies),
-        [shape(grads[0].shape, F32), shape(grads[1].shape, F32)],
+        [shape(grads[0].shape, F32), shape(grads[1].shape, F32), shape((channels, hid), F32)],
         [head_grad, *grads],
-        [pltpu.VMEM(grads[0].shape, F32), pltpu.VMEM(grads[1].shape, F32), pltpu.SemaphoreType.DMA((2,))],
-        outside=(1, 2),
-    )
-    rendered = rendered[:, :, ::RAY_SAMPLES].reshape(channels - 1, -1)
+        [pltpu.VMEM(grads[0].shape, F32), pltpu.VMEM(grads[1].shape, F32), pltpu.SemaphoreType.DMA((3,))],
+        outside=(0, 3),
+    )
     return (first_grad, hidden_grad, head_grad, rendered)
 
 

time: 61.6 us -> 57.8 us (0.938)
  local copies, waits for them, and re-layouts: 4.18 us -> 0 us
  waiting for transfers between devices: 18.5 us -> 19.9 us
    unnamed x8 -> x0, local copies, waits for them, and re-layouts: 3.44 us -> none
    all_to_all x1, waiting for transfers between devices: 1.95 us -> 3.42 us  [per_device(): lax.all_to_all(raw, 'expert', split_axis=0, concat_axis=0, tiled=True)]
    all_to_all x1, waiting for transfers between devices: 0.3 us -> 1.74 us  [per_device(): lax.all_to_all(headpart, ('expert', 'replica'), split_axis=0, concat_axis...]
    all_to_all x1, waiting for transfers between devices: 15.9 us -> 14.6 us  [per_device(): lax.all_to_all(outbound, 'expert', split_axis=0, concat_axis=0, tiled=True)]
    reshape x1 -> x0, local copies, waits for them, and re-layouts: 0.66 us -> none  [per_device(): rendered = rendered[:, :, ::RAY_SAMPLES].reshape(channels - 1, -1)]
    all_to_all x1, starting transfers between devices: 4.16 us -> 3.51 us  [per_device(): lax.all_to_all(headpart, ('expert', 'replica'), split_axis=0, concat_axis...]
    pallas_call x7 -> x8, Pallas kernels: 22.1 us -> 21.8 us  [call(): pl.pallas_call(kernel, out_shape=[(pltpu.HBM if i < outside[1] else VMEM)...]
  transfers between devices with their start and end apart: 5 -> 5, of which waited for: 4 -> 4; matrix products, arithmetic and copies ran while one was open for 1% -> 0% of each run, Pallas kernels for 14% -> 17%
where the time goes in v3:
time: 57.8 us; the launch traced here: 57.4 us
  Pallas kernels  21.8 us (38%)
  waiting for transfers between devices  19.9 us (34%)
  starting transfers between devices  15 us (26%)
  between operations  0.69 us (1%)
    pallas_call x8, Pallas kernels, call(): pl.pallas_call(kernel, out_shape=[(pltpu.HBM if i < outside[1] else VMEM)...  21.8 us
    all_to_all x1, waiting for transfers between devices, per_device(): lax.all_to_all(outbound, 'expert', split_axis=0, concat_axis=0, tiled=True)  14.6 us
    all_to_all x1, starting transfers between devices, per_device(): lax.all_to_all(outbound, 'expert', split_axis=0, concat_axis=0, tiled=True)  7.26 us
    all_to_all x1, starting transfers between devices, per_device(): lax.all_to_all(raw, 'expert', split_axis=0, concat_axis=0, tiled=True)  3.65 us
    all_to_all x1, starting transfers between devices, per_device(): lax.all_to_all(headpart, ('expert', 'replica'), split_axis=0, concat_axis...  3.51 us
    all_to_all x1, waiting for transfers between devices, per_device(): lax.all_to_all(raw, 'expert', split_axis=0, concat_axis=0, tiled=True)  3.42 us
    all_to_all x1, waiting for transfers between devices, per_device(): lax.all_to_all(headpart, ('expert', 'replica'), split_axis=0, concat_axis...  1.74 us
  transfers between devices with their start and end apart: 5, of which 4 were waited for; matrix products, arithmetic and copies ran while one was open for 0% of the time, Pallas kernels for 17%

profile of v3, /device:TPU:0, one launch (start us, length us, event | category | flops | bytes accessed | tf_op | source)
XLA Modules:
  0.0 57.4 jit_solution(5294936325241187171)
XLA Ops:
  0.6 3.2 %shard_map.120 = bf16[8,288,128]{2,1,0:T(8,128)(2,1)} custom-call(s32[8,128]{1,0:T(8,128)} %bitcast.5, bf16[1024,128]{1,0:T(8,128)(2,1)} %refs_1_.1, f32[8,128]{1,0:T(8,128)} %bitcast.6, s32[1,16]{1,0:T(1,128)} %bitcast.7, f32[3,16]{1,0:T(4,128)} %refs_4_.1, f32[3,256]{1,0:T(4,128)} %refs_5_.1), custom_call_target="tpu_custom_call" | custom-call | tf_op jit(solution)/shard_map/pallas_call | solution.py:445
  3.8 7.3 %all-to-all-start = ((bf16[8,288,128]{2,1,0:T(8,128)(2,1)}), bf16[8,288,128]{2,1,0:T(8,128)(2,1)S(1)}, u32[]{:S(2)}, u32[]{:S(2)}) async-start(bf16[8,288,128]{2,1,0:T(8,128)(2,1)} %shard_map.120), calls=%async_computation | async-start | bytes 1179648 | tf_op jit(solution)/shard_map/all_to_all | solution.py:507
  11.1 1.3 %shard_map.121 = (bf16[2,128,256]{2,1,0:T(8,128)(2,1)S(1)}, bf16[2,3,256,256]{3,2,1,0:T(8,128)(2,1)S(1)}, bf16[4,256]{1,0:T(4,128)(2,1)S(1)}) custom-call(bf16[2,128,256]{2,1,0:T(8,128)(2,1)} %first_in.1, bf16[2,3,256,256]{3,2,1,0:T(8,128)(2,1)} %hidden_in.3, bf16[4,256]{1,0:T(4,128)(2,1)} %head_in.1), custom_call_target="tpu_custom_call" | custom-call | flops 3000000000 | tf_op jit(solution)/shard_map/pallas_call | solution.py:445
  12.4 14.6 %all-to-all-done.recv_ref = bf16[8,288,128]{2,1,0:T(8,128)(2,1)S(1)} async-done(((bf16[8,288,128]{2,1,0:T(8,128)(2,1)}), bf16[8,288,128]{2,1,0:T(8,128)(2,1)S(1)}, u32[]{:S(2)}, u32[]{:S(2)}) %all-to-all-start) | async-done | bytes 589856 | tf_op jit(solution)/shard_map/all_to_all | solution.py:507
  27.0 4.7 %shard_map.122 = (bf16[3,2,1024,256]{3,2,1,0:T(8,128)(2,1)}, bf16[4,2,1024,256]{3,2,1,0:T(8,128)(2,1)}, bf16[8,64,128]{2,1,0:T(8,128)(2,1)}, bf16[2,1024,256]{2,1,0:T(8,128)(2,1)S(1)}) custom-call(bf16[8,288,128]{2,1,0:T(8,128)(2,1)S(1)} %all-to-all-done.recv_ref, bf16[2,128,256]{2,1,0:T(8,128)(2,1)S(1)} %get-tuple-element.26.first_ref, ...), custom_call_target="tpu_custom_call" | custom-call | flops 1000000000 | tf_op jit(solution)/shard_map/pallas_call | solution.py:445
  31.7 3.6 %all-to-all-start.1 = ((bf16[8,64,128]{2,1,0:T(8,128)(2,1)}), bf16[8,64,128]{2,1,0:T(8,128)(2,1)S(1)}, u32[]{:S(2)}, u32[]{:S(2)}) async-start(bf16[8,64,128]{2,1,0:T(8,128)(2,1)} %get-tuple-element.29), calls=%async_computation.1 | async-start | bytes 262144 | tf_op jit(solution)/shard_map/all_to_all | solution.py:530
  35.3 3.9 %shard_map.123 = (bf16[3,2,256,1024]{3,2,1,0:T(8,128)(2,1)}, bf16[2,128,1024]{2,1,0:T(8,128)(2,1)}, s32[8,1024]{1,0:T(8,128)S(1)}, s32[8,1024]{1,0:T(8,128)S(1)}, f32[7,64,128]{2,1,0:T(8,128)S(1)}) custom-call(bf16[3,2,1024,256]{3,2,1,0:T(8,128)(2,1)} %get-tuple-element.30.act_in, bf16[8,288,128]{2,1,0:T(8,128)(2,1)S(1)} %all-to-all-done.recv_ref), custom_call_target="tpu_custom_call" | custom-call | flops 5000000000 | tf_op jit(solution)/shard_map/pallas_call | solution.py:445
  39.3 3.4 %all-to-all-done.1.raws_ref = bf16[8,64,128]{2,1,0:T(8,128)(2,1)S(1)} async-done(((bf16[8,64,128]{2,1,0:T(8,128)(2,1)}), bf16[8,64,128]{2,1,0:T(8,128)(2,1)S(1)}, u32[]{:S(2)}, u32[]{:S(2)}) %all-to-all-start.1) | async-done | bytes 131104 | tf_op jit(solution)/shard_map/all_to_all | solution.py:530
  42.7 3.1 %shard_map.124 = (f32[3,16]{1,0:T(4,128)}, bf16[2,8,1024]{2,1,0:T(8,128)(2,1)S(1)}, f32[16,4,256]{2,1,0:T(4,128)}) custom-call(s32[1]{0:T(128)} %bitcast.me_ref, bf16[8,64,128]{2,1,0:T(8,128)(2,1)S(1)} %all-to-all-done.1.raws_ref, s32[8,1024]{1,0:T(8,128)S(1)} %get-tuple-element.31.rank_ref, s32[8,1024]{1,0:T(8,128)S(1)} %get-tuple-element.32.name_ref, ...), custom_call_target="tpu_custom_call" | custom-call | flops 1000000000 | tf_op jit(solution)/shard_map/pallas_call | solution.py:445
  45.8 3.5 %all-to-all-start.2 = ((f32[16,4,256]{2,1,0:T(4,128)}), f32[16,4,256]{2,1,0:T(4,128)S(1)}, u32[]{:S(2)}, u32[]{:S(2)}) async-start(f32[16,4,256]{2,1,0:T(4,128)} %get-tuple-element.35), calls=%async_computation.2 | async-start | bytes 131072 | tf_op jit(solution)/shard_map/all_to_all | solution.py:571
  49.3 4.5 %shard_map.126 = (f32[2,64,256]{2,1,0:T(8,128)S(1)}, f32[2,3,128,256]{3,2,1,0:T(8,128)S(1)}, f32[2,64,256]{2,1,0:T(8,128)S(1)}, f32[2,3,128,256]{3,2,1,0:T(8,128)S(1)}) custom-call(s32[1]{0:T(128)} %bitcast.4.me_ref, bf16[4,2,1024,256]{3,2,1,0:T(8,128)(2,1)} %get-tuple-element.36.slope_in, bf16[3,2,256,1024]{3,2,1,0:T(8,128)(2,1)} %get-tuple-element.37.actt_in, ...), custom_call_target="tpu_custom_call" | custom-call | flops 5000000000 | tf_op jit(solution)/shard_map/pallas_call | solution.py:445
  53.8 0.4 collective-permute-start.1
  54.2 0.2 collective-permute-start
  54.4 1.7 %all-to-all-done.2.heads_ref = f32[16,4,256]{2,1,0:T(4,128)S(1)} async-done(((f32[16,4,256]{2,1,0:T(4,128)}), f32[16,4,256]{2,1,0:T(4,128)S(1)}, u32[]{:S(2)}, u32[]{:S(2)}) %all-to-all-start.2) | async-done | bytes 65568 | tf_op jit(solution)/shard_map/all_to_all | solution.py:571
  56.2 0.2 collective-permute-done.refs_2_
  56.4 0.0 collective-permute-done.1.refs_3_
  56.4 1.0 %shard_map.127 = (f32[2,64,256]{2,1,0:T(8,128)}, f32[2,3,128,256]{3,2,1,0:T(8,128)}, f32[4,256]{1,0:T(4,128)}) custom-call(f32[4,256]{1,0:T(4,128)S(1)} %shard_map.125.head_ref, f32[2,64,256]{2,1,0:T(8,128)S(1)} %get-tuple-element.40.refs_0_, f32[2,3,128,256]{3,2,1,0:T(8,128)S(1)} %get-tuple-element.41.refs_1_, ...), custom_call_target="tpu_custom_call" | custom-call | tf_op jit(solution)/shard_map/pallas_call | solution.py:445
  (1 shorter events, 0.0 us)
Async XLA Ops:
  3.8 23.2 %all-to-all-start = ((bf16[8,288,128]{2,1,0:T(8,128)(2,1)}), bf16[8,288,128]{2,1,0:T(8,128)(2,1)S(1)}, u32[]{:S(2)}, u32[]{:S(2)}) async-start(bf16[8,288,128]{2,1,0:T(8,128)(2,1)} %shard_map.120), calls=%async_computation | async-start | bytes 1179648 | tf_op jit(solution)/shard_map/all_to_all | solution.py:507
  31.7 11.0 %all-to-all-start.1 = ((bf16[8,64,128]{2,1,0:T(8,128)(2,1)}), bf16[8,64,128]{2,1,0:T(8,128)(2,1)S(1)}, u32[]{:S(2)}, u32[]{:S(2)}) async-start(bf16[8,64,128]{2,1,0:T(8,128)(2,1)} %get-tuple-element.29), calls=%async_computation.1 | async-start | bytes 262144 | tf_op jit(solution)/shard_map/all_to_all | solution.py:530
  45.8 10.4 %all-to-all-start.2 = ((f32[16,4,256]{2,1,0:T(4,128)}), f32[16,4,256]{2,1,0:T(4,128)S(1)}, u32[]{:S(2)}, u32[]{:S(2)}) async-start(f32[16,4,256]{2,1,0:T(4,128)} %get-tuple-element.35), calls=%async_computation.2 | async-start | bytes 131072 | tf_op jit(solution)/shard_map/all_to_all | solution.py:571
  53.8 2.5 %collective-permute-start.1 = (f32[2,3,128,256]{3,2,1,0:T(8,128)S(1)}, f32[2,3,128,256]{3,2,1,0:T(8,128)S(1)}, u32[]{:S(2)}, u32[]{:S(2)}) collective-permute-start(f32[2,3,128,256]{3,2,1,0:T(8,128)S(1)} %get-tuple-element.43), channel_id=1, source_target_pairs={{0,1},{1,0},{2,3},{3,2},{4,5},{5,4},{6,7},{7,6},{8,9},{9,8},{10,11... | collective-permute-start | bytes 2359304 | tf_op jit(solution)/shard_map/ppermute | solution.py:597
  54.2 2.2 %collective-permute-start = (f32[2,64,256]{2,1,0:T(8,128)S(1)}, f32[2,64,256]{2,1,0:T(8,128)S(1)}, u32[]{:S(2)}, u32[]{:S(2)}) collective-permute-start(f32[2,64,256]{2,1,0:T(8,128)S(1)} %get-tuple-element.42), channel_id=1, source_target_pairs={{0,1},{1,0},{2,3},{3,2},{4,5},{5,4},{6,7},{7,6},{8,9},{9,8},{10,11... | collective-permute-start | bytes 393224 | tf_op jit(solution)/shard_map/ppermute | solution.py:597

commit v4 on v3

--- a/solution.py
+++ b/solution.py
@@ -67,10 +67,11 @@
     region_ref, enc_ref, spacing_ref, frame_ref, target_ref, code_ref = inside
     owners, rows = held.shape[0], held.shape[1] - META
     samples = enc_ref.shape[0]
-    for load in loads:
-        load.wait()
+    loads[0].wait()
     region = region_ref[...]
     slot = lane_row(region * capacity + ranks(region, experts))
+    for load in loads[1:]:
+        load.wait()
     enc = enc_ref[...]
 
     frames = code_ref.shape[1]
@@ -138,7 +139,6 @@
     act_out,
     slope_out,
     raw_ref,
-    act_top,
     held,
     act_ref,
     slope_ref,
@@ -155,7 +155,7 @@
 
     def saves(t, layer):
         at = rows_of(t)
-        pairs_of = [(slope_ref, slope_out)] + ([(act_ref, act_out)] if layer < layers - 1 else [])
+        pairs_of = [(slope_ref, slope_out), (act_ref, act_out)]
         return [
             pltpu.make_async_copy(a.at[layer, :, at, :], b.at[layer, :, at, :], done.at[k, layer, t])
             for k, (a, b) in enumerate(pairs_of)
@@ -172,10 +172,7 @@
                 weight = first_ref[x] if layer == 0 else hidden_ref[x, layer - 1]
                 act, slope = layer_forward(dot(current[x], weight))
                 slope_ref[layer, x, at, :] = slope
-                if layer < layers - 1:
-                    act_ref[layer, x, at, :] = act
-                else:
-                    act_top[x, at, :] = act
+                act_ref[layer, x, at, :] = act
                 current[x] = act
             for save in saves(t, layer):
                 save.start()
@@ -204,12 +201,9 @@
     same = row // RAY_SAMPLES == col // RAY_SAMPLES
 
     def along(x, mask):
-        high = x.astype(BF16)
-        rest = x - high.astype(F32)
-        mid = rest.astype(BF16)
-        low = (rest - mid.astype(F32)).astype(BF16)
-        w = hot(mask)
-        return dot(high, w) + dot(mid, w) + dot(low, w)
+        high, low = split(x)
+        both = dot(jnp.concatenate([high, low], axis=1), jnp.concatenate([hot(mask)] * 2, axis=0))
+        return both
 
     soft = jnp.maximum(raw[0], 0.0) + jnp.log1p(jnp.exp(-jnp.abs(raw[0])))
     optical = soft * spacing
@@ -233,7 +227,7 @@
 
 
 def plan_kernel(
-    local, capacity, act_in, recv_ref, actt_out, enct_out, rank_ref, name_ref, laid_ref, act_ref, actt_ref, enct_ref, moved
+    local, capacity, act_in, recv_ref, actt_out, enct_out, ranked_ref, name_ref, laid_ref, act_ref, actt_ref, enct_ref, moved
 ):
     layers = actt_ref.shape[0]
     loads = [pltpu.make_async_copy(act_in.at[k], act_ref.at[k], moved.at[0, k]) for k in range(layers)]
@@ -243,12 +237,12 @@
     sources, slots = recv_ref.shape[0], recv_ref.shape[1] - META
     rows = sources * capacity
     experts = sources * local
-    samples = rank_ref.shape[1]
+    samples = ranked_ref.shape[2]
     chunks = samples // LANES
 
     def one(s, carry):
         region = recv_ref[s, slots : slots + chunks, :].astype(F32).astype(jnp.int32)
-        rank_ref[pl.ds(s, 1), :] = lane_row(ranks(region, experts))
+        ranked_ref[s] = hot(iota((capacity, samples), 0) == lane_row(ranks(region, experts)))
         name_ref[pl.ds(s, 1), :] = lane_row(region)
         return carry
 
@@ -284,23 +278,25 @@
     local,
     capacity,
     me_ref,
+    act_in,
     raws_ref,
-    rank_ref,
+    ranked_ref,
     name_ref,
     laid_ref,
-    act_ref,
     rendered_out,
     gslot_ref,
     headpart_ref,
     wide,
     dense,
     grad,
-    ranked_ref,
+    act_ref,
     rendered_ref,
     moved,
 ):
-    save = pltpu.make_async_copy(rendered_ref, rendered_out, moved)
-    sources, samples = rank_ref.shape
+    load = pltpu.make_async_copy(act_in.at[act_in.shape[0] - 1], act_ref, moved.at[0])
+    save = pltpu.make_async_copy(rendered_ref, rendered_out, moved.at[1])
+    load.start()
+    sources, samples = ranked_ref.shape[0], ranked_ref.shape[2]
     owners, pairs = raws_ref.shape[0], raws_ref.shape[1] // sources
     channels = pairs // local
     me = me_ref[0]
@@ -312,9 +308,7 @@
         name = name_ref[pl.ds(s, 1), :]
         at = pl.ds(pl.multiple_of(s * pairs, pairs), pairs)
         block = wide[:, at, :].reshape(owners * pairs, capacity).astype(BF16)
-        pick = hot(iota((capacity, samples), 0) == rank_ref[pl.ds(s, 1), :])
-        ranked_ref[s] = pick
-        spread = dot(block, pick)
+        spread = dot(block, ranked_ref[s])
         total = jnp.zeros((pairs, samples), F32)
         for o in range(owners):
             total = total + jnp.where(name - o * local == member, spread[o * pairs : (o + 1) * pairs], 0.0)
@@ -360,6 +354,7 @@
                     axis=0,
                 )
             )
+    load.wait()
     head_total = None
     for x in range(local):
         part = jnp.concatenate(parts[x], axis=1).astype(BF16)
@@ -509,18 +504,17 @@
     tile = 4
     top = (local, rows, hid)
     lower = (layers - 1,) + top
-    acts, slopes, raw, act_top = call(
+    acts, slopes, raw = call(
         functools.partial(forward_kernel, capacity, tile),
         [
-            shape(lower, BF16),
+            shape((layers,) + top, BF16),
             shape((layers,) + top, BF16),
             shape((owners, owners * pairs, capacity), BF16),
-            shape(top, BF16),
         ],
         [recv, first_half, hidden_half, head],
         [
             pltpu.VMEM((owners * pairs, capacity), F32),
-            pltpu.VMEM(lower, BF16),
+            pltpu.VMEM((layers,) + top, BF16),
             pltpu.VMEM((layers,) + top, BF16),
             pltpu.SemaphoreType.DMA((2, layers, owners // tile)),
         ],
@@ -529,12 +523,12 @@
     )
     raws = lax.all_to_all(raw, "expert", split_axis=0, concat_axis=0, tiled=True)
     flipped = (layers - 1, local, hid, rows)
-    actt, enct, order, names, laid = call(
+    actt, enct, ranked, names, laid = call(
         functools.partial(plan_kernel, local, capacity),
         [
             shape(flipped, BF16),
             shape((local, enc_width, rows), BF16),
-            shape((owners, samples), jnp.int32),
+            shape((owners, capacity, samples), BF16),
             shape((owners, samples), jnp.int32),
             shape((2 * channels - 1, owners * chunks, LANES), F32),
         ],
@@ -555,17 +549,17 @@
             shape((local, 2 * channels, rows), BF16),
             shape((owners * copies, channels, hid), F32),
         ],
-        [owner, raws, order, names, laid, act_top],
+        [owner, acts, raws, ranked, names, laid],
         [
             pltpu.VMEM((owners, owners * pairs, capacity), F32),
             pltpu.VMEM((channels, owners * chunks, LANES), F32),
             pltpu.VMEM((channels, owners * chunks, LANES), F32),
-            pltpu.VMEM((owners, capacity, samples), BF16),
+            pltpu.VMEM(top, BF16),
             pltpu.VMEM(target_rgb.shape, F32),
-            pltpu.SemaphoreType.DMA,
+            pltpu.SemaphoreType.DMA((2,)),
         ],
         scalars=1,
-        outside=(0, 1),
+        outside=(1, 1),
         flops=10**9,
     )
     heads = lax.all_to_all(headpart, ("expert", "replica"), split_axis=0, concat_axis=0, tiled=True)

time: 57.8 us -> 57.6 us (level)
  transfers between devices with their start and end apart: 5 -> 5, of which waited for: 4 -> 4; matrix products, arithmetic and copies ran while one was open for 0% -> 0% of each run, Pallas kernels for 17% -> 18%
where the time goes in v4:
time: 57.6 us; the launch traced here: 57.2 us
  Pallas kernels  21.8 us (38%)
  waiting for transfers between devices  19.7 us (34%)
  starting transfers between devices  15 us (26%)
  between operations  0.69 us (1%)
    pallas_call x8, Pallas kernels, call(): pl.pallas_call(kernel, out_shape=[(pltpu.HBM if i < outside[1] else VMEM)...  21.8 us
    all_to_all x1, waiting for transfers between devices, per_device(): lax.all_to_all(outbound, 'expert', split_axis=0, concat_axis=0, tiled=True)  14.6 us
    all_to_all x1, starting transfers between devices, per_device(): lax.all_to_all(outbound, 'expert', split_axis=0, concat_axis=0, tiled=True)  7.25 us
    all_to_all x1, starting transfers between devices, per_device(): lax.all_to_all(raw, 'expert', split_axis=0, concat_axis=0, tiled=True)  3.65 us
    all_to_all x1, starting transfers between devices, per_device(): lax.all_to_all(headpart, ('expert', 'replica'), split_axis=0, concat_axis...  3.51 us
    all_to_all x1, waiting for transfers between devices, per_device(): lax.all_to_all(raw, 'expert', split_axis=0, concat_axis=0, tiled=True)  3.16 us
    all_to_all x1, waiting for transfers between devices, per_device(): lax.all_to_all(headpart, ('expert', 'replica'), split_axis=0, concat_axis...  1.74 us
  transfers between devices with their start and end apart: 5, of which 4 were waited for; matrix products, arithmetic and copies ran while one was open for 0% of the time, Pallas kernels for 18%

profile of v4, /device:TPU:0, one launch (start us, length us, event | category | flops | bytes accessed | tf_op | source)
XLA Modules:
  0.0 57.2 jit_solution(9378111782037092880)
XLA Ops:
  0.6 3.1 %shard_map.120 = bf16[8,288,128]{2,1,0:T(8,128)(2,1)} custom-call(s32[8,128]{1,0:T(8,128)} %bitcast.5, bf16[1024,128]{1,0:T(8,128)(2,1)} %refs_1_.1, f32[8,128]{1,0:T(8,128)} %bitcast.6, s32[1,16]{1,0:T(1,128)} %bitcast.7, f32[3,16]{1,0:T(4,128)} %refs_4_.1, f32[3,256]{1,0:T(4,128)} %refs_5_.1), custom_call_target="tpu_custom_call" | custom-call | tf_op jit(solution)/shard_map/pallas_call | solution.py:440
  3.7 7.3 %all-to-all-start = ((bf16[8,288,128]{2,1,0:T(8,128)(2,1)}), bf16[8,288,128]{2,1,0:T(8,128)(2,1)S(1)}, u32[]{:S(2)}, u32[]{:S(2)}) async-start(bf16[8,288,128]{2,1,0:T(8,128)(2,1)} %shard_map.120), calls=%async_computation | async-start | bytes 1179648 | tf_op jit(solution)/shard_map/all_to_all | solution.py:502
  10.9 1.3 %shard_map.121 = (bf16[2,128,256]{2,1,0:T(8,128)(2,1)S(1)}, bf16[2,3,256,256]{3,2,1,0:T(8,128)(2,1)S(1)}, bf16[4,256]{1,0:T(4,128)(2,1)S(1)}) custom-call(bf16[2,128,256]{2,1,0:T(8,128)(2,1)} %first_in.1, bf16[2,3,256,256]{3,2,1,0:T(8,128)(2,1)} %hidden_in.3, bf16[4,256]{1,0:T(4,128)(2,1)} %head_in.1), custom_call_target="tpu_custom_call" | custom-call | flops 3000000000 | tf_op jit(solution)/shard_map/pallas_call | solution.py:440
  12.3 14.6 %all-to-all-done.recv_ref = bf16[8,288,128]{2,1,0:T(8,128)(2,1)S(1)} async-done(((bf16[8,288,128]{2,1,0:T(8,128)(2,1)}), bf16[8,288,128]{2,1,0:T(8,128)(2,1)S(1)}, u32[]{:S(2)}, u32[]{:S(2)}) %all-to-all-start) | async-done | bytes 589856 | tf_op jit(solution)/shard_map/all_to_all | solution.py:502
  26.8 4.7 %shard_map.122 = (bf16[4,2,1024,256]{3,2,1,0:T(8,128)(2,1)}, bf16[4,2,1024,256]{3,2,1,0:T(8,128)(2,1)}, bf16[8,64,128]{2,1,0:T(8,128)(2,1)}) custom-call(bf16[8,288,128]{2,1,0:T(8,128)(2,1)S(1)} %all-to-all-done.recv_ref, bf16[2,128,256]{2,1,0:T(8,128)(2,1)S(1)} %get-tuple-element.25.first_ref, bf16[2,3,256,256]{3,2,1,0:T(8,128)(2,1)S(1)} %get-tuple-element.26.hidden_ref, ...), custom_call_target="tpu_custom_call" | custom-call | flops 1000000000 | tf_op jit(solution)/shard_map/pallas_call | solution.py:440
  31.6 3.6 %all-to-all-start.1 = ((bf16[8,64,128]{2,1,0:T(8,128)(2,1)}), bf16[8,64,128]{2,1,0:T(8,128)(2,1)S(1)}, u32[]{:S(2)}, u32[]{:S(2)}) async-start(bf16[8,64,128]{2,1,0:T(8,128)(2,1)} %get-tuple-element.29), calls=%async_computation.1 | async-start | bytes 262144 | tf_op jit(solution)/shard_map/all_to_all | solution.py:524
  35.2 4.2 %shard_map.123 = (bf16[3,2,256,1024]{3,2,1,0:T(8,128)(2,1)}, bf16[2,128,1024]{2,1,0:T(8,128)(2,1)}, bf16[8,128,1024]{2,1,0:T(8,128)(2,1)S(1)}, s32[8,1024]{1,0:T(8,128)S(1)}, f32[7,64,128]{2,1,0:T(8,128)S(1)}) custom-call(bf16[4,2,1024,256]{3,2,1,0:T(8,128)(2,1)} %get-tuple-element.28.act_in, bf16[8,288,128]{2,1,0:T(8,128)(2,1)S(1)} %all-to-all-done.recv_ref), custom_call_target="tpu_custom_call" | custom-call | flops 5000000000 | tf_op jit(solution)/shard_map/pallas_call | solution.py:440
  39.4 3.2 %all-to-all-done.1.raws_ref = bf16[8,64,128]{2,1,0:T(8,128)(2,1)S(1)} async-done(((bf16[8,64,128]{2,1,0:T(8,128)(2,1)}), bf16[8,64,128]{2,1,0:T(8,128)(2,1)S(1)}, u32[]{:S(2)}, u32[]{:S(2)}) %all-to-all-start.1) | async-done | bytes 131104 | tf_op jit(solution)/shard_map/all_to_all | solution.py:524
  42.6 3.0 %shard_map.124 = (f32[3,16]{1,0:T(4,128)}, bf16[2,8,1024]{2,1,0:T(8,128)(2,1)S(1)}, f32[16,4,256]{2,1,0:T(4,128)}) custom-call(s32[1]{0:T(128)} %bitcast.me_ref, bf16[4,2,1024,256]{3,2,1,0:T(8,128)(2,1)} %get-tuple-element.28.act_in, bf16[8,64,128]{2,1,0:T(8,128)(2,1)S(1)} %all-to-all-done.1.raws_ref, ...), custom_call_target="tpu_custom_call" | custom-call | flops 1000000000 | tf_op jit(solution)/shard_map/pallas_call | solution.py:440
  45.5 3.5 %all-to-all-start.2 = ((f32[16,4,256]{2,1,0:T(4,128)}), f32[16,4,256]{2,1,0:T(4,128)S(1)}, u32[]{:S(2)}, u32[]{:S(2)}) async-start(f32[16,4,256]{2,1,0:T(4,128)} %get-tuple-element.33), calls=%async_computation.2 | async-start | bytes 131072 | tf_op jit(solution)/shard_map/all_to_all | solution.py:565
  49.1 4.5 %shard_map.126 = (f32[2,64,256]{2,1,0:T(8,128)S(1)}, f32[2,3,128,256]{3,2,1,0:T(8,128)S(1)}, f32[2,64,256]{2,1,0:T(8,128)S(1)}, f32[2,3,128,256]{3,2,1,0:T(8,128)S(1)}) custom-call(s32[1]{0:T(128)} %bitcast.4.me_ref, bf16[4,2,1024,256]{3,2,1,0:T(8,128)(2,1)} %get-tuple-element.34.slope_in, bf16[3,2,256,1024]{3,2,1,0:T(8,128)(2,1)} %get-tuple-element.35.actt_in, ...), custom_call_target="tpu_custom_call" | custom-call | flops 5000000000 | tf_op jit(solution)/shard_map/pallas_call | solution.py:440
  53.6 0.4 collective-permute-start.1
  54.0 0.2 collective-permute-start
  54.2 1.7 %all-to-all-done.2.heads_ref = f32[16,4,256]{2,1,0:T(4,128)S(1)} async-done(((f32[16,4,256]{2,1,0:T(4,128)}), f32[16,4,256]{2,1,0:T(4,128)S(1)}, u32[]{:S(2)}, u32[]{:S(2)}) %all-to-all-start.2) | async-done | bytes 65568 | tf_op jit(solution)/shard_map/all_to_all | solution.py:565
  55.9 0.2 collective-permute-done.refs_2_
  56.2 0.0 collective-permute-done.1.refs_3_
  56.2 1.0 %shard_map.127 = (f32[2,64,256]{2,1,0:T(8,128)}, f32[2,3,128,256]{3,2,1,0:T(8,128)}, f32[4,256]{1,0:T(4,128)}) custom-call(f32[4,256]{1,0:T(4,128)S(1)} %shard_map.125.head_ref, f32[2,64,256]{2,1,0:T(8,128)S(1)} %get-tuple-element.38.refs_0_, f32[2,3,128,256]{3,2,1,0:T(8,128)S(1)} %get-tuple-element.39.refs_1_, ...), custom_call_target="tpu_custom_call" | custom-call | tf_op jit(solution)/shard_map/pallas_call | solution.py:440
  (1 shorter events, 0.0 us)
Async XLA Ops:
  3.7 23.1 %all-to-all-start = ((bf16[8,288,128]{2,1,0:T(8,128)(2,1)}), bf16[8,288,128]{2,1,0:T(8,128)(2,1)S(1)}, u32[]{:S(2)}, u32[]{:S(2)}) async-start(bf16[8,288,128]{2,1,0:T(8,128)(2,1)} %shard_map.120), calls=%async_computation | async-start | bytes 1179648 | tf_op jit(solution)/shard_map/all_to_all | solution.py:502
  31.6 11.0 %all-to-all-start.1 = ((bf16[8,64,128]{2,1,0:T(8,128)(2,1)}), bf16[8,64,128]{2,1,0:T(8,128)(2,1)S(1)}, u32[]{:S(2)}, u32[]{:S(2)}) async-start(bf16[8,64,128]{2,1,0:T(8,128)(2,1)} %get-tuple-element.29), calls=%async_computation.1 | async-start | bytes 262144 | tf_op jit(solution)/shard_map/all_to_all | solution.py:524
  45.5 10.4 %all-to-all-start.2 = ((f32[16,4,256]{2,1,0:T(4,128)}), f32[16,4,256]{2,1,0:T(4,128)S(1)}, u32[]{:S(2)}, u32[]{:S(2)}) async-start(f32[16,4,256]{2,1,0:T(4,128)} %get-tuple-element.33), calls=%async_computation.2 | async-start | bytes 131072 | tf_op jit(solution)/shard_map/all_to_all | solution.py:565
  53.6 2.5 %collective-permute-start.1 = (f32[2,3,128,256]{3,2,1,0:T(8,128)S(1)}, f32[2,3,128,256]{3,2,1,0:T(8,128)S(1)}, u32[]{:S(2)}, u32[]{:S(2)}) collective-permute-start(f32[2,3,128,256]{3,2,1,0:T(8,128)S(1)} %get-tuple-element.41), channel_id=1, source_target_pairs={{0,1},{1,0},{2,3},{3,2},{4,5},{5,4},{6,7},{7,6},{8,9},{9,8},{10,11... | collective-permute-start | bytes 2359304 | tf_op jit(solution)/shard_map/ppermute | solution.py:591
  54.0 2.2 %collective-permute-start = (f32[2,64,256]{2,1,0:T(8,128)S(1)}, f32[2,64,256]{2,1,0:T(8,128)S(1)}, u32[]{:S(2)}, u32[]{:S(2)}) collective-permute-start(f32[2,64,256]{2,1,0:T(8,128)S(1)} %get-tuple-element.40), channel_id=1, source_target_pairs={{0,1},{1,0},{2,3},{3,2},{4,5},{5,4},{6,7},{7,6},{8,9},{9,8},{10,11... | collective-permute-start | bytes 393224 | tf_op jit(solution)/shard_map/ppermute | solution.py:591

commit v5 on v4

--- a/solution.py
+++ b/solution.py
@@ -241,7 +241,7 @@
     chunks = samples // LANES
 
     def one(s, carry):
-        region = recv_ref[s, slots : slots + chunks, :].astype(F32).astype(jnp.int32)
+        region = recv_ref[s, slots:, :].astype(F32)[:chunks].astype(jnp.int32)
         ranked_ref[s] = hot(iota((capacity, samples), 0) == lane_row(ranks(region, experts)))
         name_ref[pl.ds(s, 1), :] = lane_row(region)
         return carry

time: 57.6 us -> 57.6 us (level)
  no operation moved by 1% of the time
where the time goes in v5:
time: 57.6 us; the launch traced here: 57.2 us
  Pallas kernels  21.8 us (38%)
  waiting for transfers between devices  19.7 us (34%)
  starting transfers between devices  15 us (26%)
  between operations  0.69 us (1%)
    pallas_call x8, Pallas kernels, call(): pl.pallas_call(kernel, out_shape=[(pltpu.HBM if i < outside[1] else VMEM)...  21.8 us
    all_to_all x1, waiting for transfers between devices, per_device(): lax.all_to_all(outbound, 'expert', split_axis=0, concat_axis=0, tiled=True)  14.6 us
    all_to_all x1, starting transfers between devices, per_device(): lax.all_to_all(outbound, 'expert', split_axis=0, concat_axis=0, tiled=True)  7.25 us
    all_to_all x1, starting transfers between devices, per_device(): lax.all_to_all(raw, 'expert', split_axis=0, concat_axis=0, tiled=True)  3.65 us
    all_to_all x1, starting transfers between devices, per_device(): lax.all_to_all(headpart, ('expert', 'replica'), split_axis=0, concat_axis...  3.51 us
    all_to_all x1, waiting for transfers between devices, per_device(): lax.all_to_all(raw, 'expert', split_axis=0, concat_axis=0, tiled=True)  3.16 us
    all_to_all x1, waiting for transfers between devices, per_device(): lax.all_to_all(headpart, ('expert', 'replica'), split_axis=0, concat_axis...  1.74 us
  transfers between devices with their start and end apart: 5, of which 4 were waited for; matrix products, arithmetic and copies ran while one was open for 0% of the time, Pallas kernels for 18%

profile of v5, /device:TPU:0, one launch (start us, length us, event | category | flops | bytes accessed | tf_op | source)
XLA Modules:
  0.0 57.2 jit_solution(9378111782037092880)
XLA Ops:
  0.6 3.1 %shard_map.120 = bf16[8,288,128]{2,1,0:T(8,128)(2,1)} custom-call(s32[8,128]{1,0:T(8,128)} %bitcast.5, bf16[1024,128]{1,0:T(8,128)(2,1)} %refs_1_.1, f32[8,128]{1,0:T(8,128)} %bitcast.6, s32[1,16]{1,0:T(1,128)} %bitcast.7, f32[3,16]{1,0:T(4,128)} %refs_4_.1, f32[3,256]{1,0:T(4,128)} %refs_5_.1), custom_call_target="tpu_custom_call" | custom-call | tf_op jit(solution)/shard_map/pallas_call | solution.py:440
  3.7 7.3 %all-to-all-start = ((bf16[8,288,128]{2,1,0:T(8,128)(2,1)}), bf16[8,288,128]{2,1,0:T(8,128)(2,1)S(1)}, u32[]{:S(2)}, u32[]{:S(2)}) async-start(bf16[8,288,128]{2,1,0:T(8,128)(2,1)} %shard_map.120), calls=%async_computation | async-start | bytes 1179648 | tf_op jit(solution)/shard_map/all_to_all | solution.py:502
  10.9 1.3 %shard_map.121 = (bf16[2,128,256]{2,1,0:T(8,128)(2,1)S(1)}, bf16[2,3,256,256]{3,2,1,0:T(8,128)(2,1)S(1)}, bf16[4,256]{1,0:T(4,128)(2,1)S(1)}) custom-call(bf16[2,128,256]{2,1,0:T(8,128)(2,1)} %first_in.1, bf16[2,3,256,256]{3,2,1,0:T(8,128)(2,1)} %hidden_in.3, bf16[4,256]{1,0:T(4,128)(2,1)} %head_in.1), custom_call_target="tpu_custom_call" | custom-call | flops 3000000000 | tf_op jit(solution)/shard_map/pallas_call | solution.py:440
  12.3 14.6 %all-to-all-done.recv_ref = bf16[8,288,128]{2,1,0:T(8,128)(2,1)S(1)} async-done(((bf16[8,288,128]{2,1,0:T(8,128)(2,1)}), bf16[8,288,128]{2,1,0:T(8,128)(2,1)S(1)}, u32[]{:S(2)}, u32[]{:S(2)}) %all-to-all-start) | async-done | bytes 589856 | tf_op jit(solution)/shard_map/all_to_all | solution.py:502
  26.8 4.7 %shard_map.122 = (bf16[4,2,1024,256]{3,2,1,0:T(8,128)(2,1)}, bf16[4,2,1024,256]{3,2,1,0:T(8,128)(2,1)}, bf16[8,64,128]{2,1,0:T(8,128)(2,1)}) custom-call(bf16[8,288,128]{2,1,0:T(8,128)(2,1)S(1)} %all-to-all-done.recv_ref, bf16[2,128,256]{2,1,0:T(8,128)(2,1)S(1)} %get-tuple-element.25.first_ref, bf16[2,3,256,256]{3,2,1,0:T(8,128)(2,1)S(1)} %get-tuple-element.26.hidden_ref, ...), custom_call_target="tpu_custom_call" | custom-call | flops 1000000000 | tf_op jit(solution)/shard_map/pallas_call | solution.py:440
  31.6 3.6 %all-to-all-start.1 = ((bf16[8,64,128]{2,1,0:T(8,128)(2,1)}), bf16[8,64,128]{2,1,0:T(8,128)(2,1)S(1)}, u32[]{:S(2)}, u32[]{:S(2)}) async-start(bf16[8,64,128]{2,1,0:T(8,128)(2,1)} %get-tuple-element.29), calls=%async_computation.1 | async-start | bytes 262144 | tf_op jit(solution)/shard_map/all_to_all | solution.py:524
  35.2 4.2 %shard_map.123 = (bf16[3,2,256,1024]{3,2,1,0:T(8,128)(2,1)}, bf16[2,128,1024]{2,1,0:T(8,128)(2,1)}, bf16[8,128,1024]{2,1,0:T(8,128)(2,1)S(1)}, s32[8,1024]{1,0:T(8,128)S(1)}, f32[7,64,128]{2,1,0:T(8,128)S(1)}) custom-call(bf16[4,2,1024,256]{3,2,1,0:T(8,128)(2,1)} %get-tuple-element.28.act_in, bf16[8,288,128]{2,1,0:T(8,128)(2,1)S(1)} %all-to-all-done.recv_ref), custom_call_target="tpu_custom_call" | custom-call | flops 5000000000 | tf_op jit(solution)/shard_map/pallas_call | solution.py:440
  39.4 3.2 %all-to-all-done.1.raws_ref = bf16[8,64,128]{2,1,0:T(8,128)(2,1)S(1)} async-done(((bf16[8,64,128]{2,1,0:T(8,128)(2,1)}), bf16[8,64,128]{2,1,0:T(8,128)(2,1)S(1)}, u32[]{:S(2)}, u32[]{:S(2)}) %all-to-all-start.1) | async-done | bytes 131104 | tf_op jit(solution)/shard_map/all_to_all | solution.py:524
  42.6 3.0 %shard_map.124 = (f32[3,16]{1,0:T(4,128)}, bf16[2,8,1024]{2,1,0:T(8,128)(2,1)S(1)}, f32[16,4,256]{2,1,0:T(4,128)}) custom-call(s32[1]{0:T(128)} %bitcast.me_ref, bf16[4,2,1024,256]{3,2,1,0:T(8,128)(2,1)} %get-tuple-element.28.act_in, bf16[8,64,128]{2,1,0:T(8,128)(2,1)S(1)} %all-to-all-done.1.raws_ref, ...), custom_call_target="tpu_custom_call" | custom-call | flops 1000000000 | tf_op jit(solution)/shard_map/pallas_call | solution.py:440
  45.5 3.5 %all-to-all-start.2 = ((f32[16,4,256]{2,1,0:T(4,128)}), f32[16,4,256]{2,1,0:T(4,128)S(1)}, u32[]{:S(2)}, u32[]{:S(2)}) async-start(f32[16,4,256]{2,1,0:T(4,128)} %get-tuple-element.33), calls=%async_computation.2 | async-start | bytes 131072 | tf_op jit(solution)/shard_map/all_to_all | solution.py:565
  49.1 4.5 %shard_map.126 = (f32[2,64,256]{2,1,0:T(8,128)S(1)}, f32[2,3,128,256]{3,2,1,0:T(8,128)S(1)}, f32[2,64,256]{2,1,0:T(8,128)S(1)}, f32[2,3,128,256]{3,2,1,0:T(8,128)S(1)}) custom-call(s32[1]{0:T(128)} %bitcast.4.me_ref, bf16[4,2,1024,256]{3,2,1,0:T(8,128)(2,1)} %get-tuple-element.34.slope_in, bf16[3,2,256,1024]{3,2,1,0:T(8,128)(2,1)} %get-tuple-element.35.actt_in, ...), custom_call_target="tpu_custom_call" | custom-call | flops 5000000000 | tf_op jit(solution)/shard_map/pallas_call | solution.py:440
  53.6 0.4 collective-permute-start.1
  54.0 0.2 collective-permute-start
  54.2 1.7 %all-to-all-done.2.heads_ref = f32[16,4,256]{2,1,0:T(4,128)S(1)} async-done(((f32[16,4,256]{2,1,0:T(4,128)}), f32[16,4,256]{2,1,0:T(4,128)S(1)}, u32[]{:S(2)}, u32[]{:S(2)}) %all-to-all-start.2) | async-done | bytes 65568 | tf_op jit(solution)/shard_map/all_to_all | solution.py:565
  55.9 0.2 collective-permute-done.refs_2_
  56.2 0.0 collective-permute-done.1.refs_3_
  56.2 1.0 %shard_map.127 = (f32[2,64,256]{2,1,0:T(8,128)}, f32[2,3,128,256]{3,2,1,0:T(8,128)}, f32[4,256]{1,0:T(4,128)}) custom-call(f32[4,256]{1,0:T(4,128)S(1)} %shard_map.125.head_ref, f32[2,64,256]{2,1,0:T(8,128)S(1)} %get-tuple-element.38.refs_0_, f32[2,3,128,256]{3,2,1,0:T(8,128)S(1)} %get-tuple-element.39.refs_1_, ...), custom_call_target="tpu_custom_call" | custom-call | tf_op jit(solution)/shard_map/pallas_call | solution.py:440
  (1 shorter events, 0.0 us)
Async XLA Ops:
  3.7 23.1 %all-to-all-start = ((bf16[8,288,128]{2,1,0:T(8,128)(2,1)}), bf16[8,288,128]{2,1,0:T(8,128)(2,1)S(1)}, u32[]{:S(2)}, u32[]{:S(2)}) async-start(bf16[8,288,128]{2,1,0:T(8,128)(2,1)} %shard_map.120), calls=%async_computation | async-start | bytes 1179648 | tf_op jit(solution)/shard_map/all_to_all | solution.py:502
  31.6 11.0 %all-to-all-start.1 = ((bf16[8,64,128]{2,1,0:T(8,128)(2,1)}), bf16[8,64,128]{2,1,0:T(8,128)(2,1)S(1)}, u32[]{:S(2)}, u32[]{:S(2)}) async-start(bf16[8,64,128]{2,1,0:T(8,128)(2,1)} %get-tuple-element.29), calls=%async_computation.1 | async-start | bytes 262144 | tf_op jit(solution)/shard_map/all_to_all | solution.py:524
  45.5 10.4 %all-to-all-start.2 = ((f32[16,4,256]{2,1,0:T(4,128)}), f32[16,4,256]{2,1,0:T(4,128)S(1)}, u32[]{:S(2)}, u32[]{:S(2)}) async-start(f32[16,4,256]{2,1,0:T(4,128)} %get-tuple-element.33), calls=%async_computation.2 | async-start | bytes 131072 | tf_op jit(solution)/shard_map/all_to_all | solution.py:565
  53.6 2.5 %collective-permute-start.1 = (f32[2,3,128,256]{3,2,1,0:T(8,128)S(1)}, f32[2,3,128,256]{3,2,1,0:T(8,128)S(1)}, u32[]{:S(2)}, u32[]{:S(2)}) collective-permute-start(f32[2,3,128,256]{3,2,1,0:T(8,128)S(1)} %get-tuple-element.41), channel_id=1, source_target_pairs={{0,1},{1,0},{2,3},{3,2},{4,5},{5,4},{6,7},{7,6},{8,9},{9,8},{10,11... | collective-permute-start | bytes 2359304 | tf_op jit(solution)/shard_map/ppermute | solution.py:591
  54.0 2.2 %collective-permute-start = (f32[2,64,256]{2,1,0:T(8,128)S(1)}, f32[2,64,256]{2,1,0:T(8,128)S(1)}, u32[]{:S(2)}, u32[]{:S(2)}) collective-permute-start(f32[2,64,256]{2,1,0:T(8,128)S(1)} %get-tuple-element.40), channel_id=1, source_target_pairs={{0,1},{1,0},{2,3},{3,2},{4,5},{5,4},{6,7},{7,6},{8,9},{9,8},{10,11... | collective-permute-start | bytes 393224 | tf_op jit(solution)/shard_map/ppermute | solution.py:591

commit v6 on v5

--- a/solution.py
+++ b/solution.py
@@ -315,9 +315,10 @@
         flat = total[:channels]
         for x in range(1, local):
             flat = flat + total[x * channels : (x + 1) * channels]
-        for k in range(chunks):
-            for c in range(channels):
-                dense[c, pl.ds(s * chunks + k, 1), :] = flat[c : c + 1, k * LANES : (k + 1) * LANES]
+        rows = pl.ds(pl.multiple_of(s * chunks, chunks), chunks)
+        for c in range(channels):
+            pieces = [flat[c : c + 1, k * LANES : (k + 1) * LANES] for k in range(chunks)]
+            dense[c, rows, :] = jnp.concatenate(pieces, axis=0)
         return carry
 
     lax.fori_loop(0, sources, unslot, 0, unroll=4)

time: 57.6 us -> 57.7 us (level)
  no operation moved by 1% of the time
where the time goes in v6:
time: 57.7 us; the launch traced here: 57.3 us
  Pallas kernels  21.9 us (38%)
  waiting for transfers between devices  19.7 us (34%)
  starting transfers between devices  15 us (26%)
  between operations  0.69 us (1%)
    pallas_call x8, Pallas kernels, call(): pl.pallas_call(kernel, out_shape=[(pltpu.HBM if i < outside[1] else VMEM)...  21.9 us
    all_to_all x1, waiting for transfers between devices, per_device(): lax.all_to_all(outbound, 'expert', split_axis=0, concat_axis=0, tiled=True)  14.6 us
    all_to_all x1, starting transfers between devices, per_device(): lax.all_to_all(outbound, 'expert', split_axis=0, concat_axis=0, tiled=True)  7.25 us
    all_to_all x1, starting transfers between devices, per_device(): lax.all_to_all(raw, 'expert', split_axis=0, concat_axis=0, tiled=True)  3.65 us
    all_to_all x1, starting transfers between devices, per_device(): lax.all_to_all(headpart, ('expert', 'replica'), split_axis=0, concat_axis...  3.51 us
    all_to_all x1, waiting for transfers between devices, per_device(): lax.all_to_all(raw, 'expert', split_axis=0, concat_axis=0, tiled=True)  3.16 us
    all_to_all x1, waiting for transfers between devices, per_device(): lax.all_to_all(headpart, ('expert', 'replica'), split_axis=0, concat_axis...  1.73 us
  transfers between devices with their start and end apart: 5, of which 4 were waited for; matrix products, arithmetic and copies ran while one was open for 0% of the time, Pallas kernels for 18%

profile of v6, /device:TPU:0, one launch (start us, length us, event | category | flops | bytes accessed | tf_op | source)
XLA Modules:
  0.0 57.3 jit_solution(6286362345311026464)
XLA Ops:
  0.6 3.1 %shard_map.120 = bf16[8,288,128]{2,1,0:T(8,128)(2,1)} custom-call(s32[8,128]{1,0:T(8,128)} %bitcast.5, bf16[1024,128]{1,0:T(8,128)(2,1)} %refs_1_.1, f32[8,128]{1,0:T(8,128)} %bitcast.6, s32[1,16]{1,0:T(1,128)} %bitcast.7, f32[3,16]{1,0:T(4,128)} %refs_4_.1, f32[3,256]{1,0:T(4,128)} %refs_5_.1), custom_call_target="tpu_custom_call" | custom-call | tf_op jit(solution)/shard_map/pallas_call | solution.py:441
  3.7 7.3 %all-to-all-start = ((bf16[8,288,128]{2,1,0:T(8,128)(2,1)}), bf16[8,288,128]{2,1,0:T(8,128)(2,1)S(1)}, u32[]{:S(2)}, u32[]{:S(2)}) async-start(bf16[8,288,128]{2,1,0:T(8,128)(2,1)} %shard_map.120), calls=%async_computation | async-start | bytes 1179648 | tf_op jit(solution)/shard_map/all_to_all | solution.py:503
  10.9 1.3 %shard_map.121 = (bf16[2,128,256]{2,1,0:T(8,128)(2,1)S(1)}, bf16[2,3,256,256]{3,2,1,0:T(8,128)(2,1)S(1)}, bf16[4,256]{1,0:T(4,128)(2,1)S(1)}) custom-call(bf16[2,128,256]{2,1,0:T(8,128)(2,1)} %first_in.1, bf16[2,3,256,256]{3,2,1,0:T(8,128)(2,1)} %hidden_in.3, bf16[4,256]{1,0:T(4,128)(2,1)} %head_in.1), custom_call_target="tpu_custom_call" | custom-call | flops 3000000000 | tf_op jit(solution)/shard_map/pallas_call | solution.py:441
  12.3 14.6 %all-to-all-done.recv_ref = bf16[8,288,128]{2,1,0:T(8,128)(2,1)S(1)} async-done(((bf16[8,288,128]{2,1,0:T(8,128)(2,1)}), bf16[8,288,128]{2,1,0:T(8,128)(2,1)S(1)}, u32[]{:S(2)}, u32[]{:S(2)}) %all-to-all-start) | async-done | bytes 589856 | tf_op jit(solution)/shard_map/all_to_all | solution.py:503
  26.8 4.7 %shard_map.122 = (bf16[4,2,1024,256]{3,2,1,0:T(8,128)(2,1)}, bf16[4,2,1024,256]{3,2,1,0:T(8,128)(2,1)}, bf16[8,64,128]{2,1,0:T(8,128)(2,1)}) custom-call(bf16[8,288,128]{2,1,0:T(8,128)(2,1)S(1)} %all-to-all-done.recv_ref, bf16[2,128,256]{2,1,0:T(8,128)(2,1)S(1)} %get-tuple-element.25.first_ref, bf16[2,3,256,256]{3,2,1,0:T(8,128)(2,1)S(1)} %get-tuple-element.26.hidden_ref, ...), custom_call_target="tpu_custom_call" | custom-call | flops 1000000000 | tf_op jit(solution)/shard_map/pallas_call | solution.py:441
  31.6 3.6 %all-to-all-start.1 = ((bf16[8,64,128]{2,1,0:T(8,128)(2,1)}), bf16[8,64,128]{2,1,0:T(8,128)(2,1)S(1)}, u32[]{:S(2)}, u32[]{:S(2)}) async-start(bf16[8,64,128]{2,1,0:T(8,128)(2,1)} %get-tuple-element.29), calls=%async_computation.1 | async-start | bytes 262144 | tf_op jit(solution)/shard_map/all_to_all | solution.py:525
  35.2 4.2 %shard_map.123 = (bf16[3,2,256,1024]{3,2,1,0:T(8,128)(2,1)}, bf16[2,128,1024]{2,1,0:T(8,128)(2,1)}, bf16[8,128,1024]{2,1,0:T(8,128)(2,1)S(1)}, s32[8,1024]{1,0:T(8,128)S(1)}, f32[7,64,128]{2,1,0:T(8,128)S(1)}) custom-call(bf16[4,2,1024,256]{3,2,1,0:T(8,128)(2,1)} %get-tuple-element.28.act_in, bf16[8,288,128]{2,1,0:T(8,128)(2,1)S(1)} %all-to-all-done.recv_ref), custom_call_target="tpu_custom_call" | custom-call | flops 5000000000 | tf_op jit(solution)/shard_map/pallas_call | solution.py:441
  39.4 3.2 %all-to-all-done.1.raws_ref = bf16[8,64,128]{2,1,0:T(8,128)(2,1)S(1)} async-done(((bf16[8,64,128]{2,1,0:T(8,128)(2,1)}), bf16[8,64,128]{2,1,0:T(8,128)(2,1)S(1)}, u32[]{:S(2)}, u32[]{:S(2)}) %all-to-all-start.1) | async-done | bytes 131104 | tf_op jit(solution)/shard_map/all_to_all | solution.py:525
  42.6 3.0 %shard_map.124 = (f32[3,16]{1,0:T(4,128)}, bf16[2,8,1024]{2,1,0:T(8,128)(2,1)S(1)}, f32[16,4,256]{2,1,0:T(4,128)}) custom-call(s32[1]{0:T(128)} %bitcast.me_ref, bf16[4,2,1024,256]{3,2,1,0:T(8,128)(2,1)} %get-tuple-element.28.act_in, bf16[8,64,128]{2,1,0:T(8,128)(2,1)S(1)} %all-to-all-done.1.raws_ref, ...), custom_call_target="tpu_custom_call" | custom-call | flops 1000000000 | tf_op jit(solution)/shard_map/pallas_call | solution.py:441
  45.6 3.5 %all-to-all-start.2 = ((f32[16,4,256]{2,1,0:T(4,128)}), f32[16,4,256]{2,1,0:T(4,128)S(1)}, u32[]{:S(2)}, u32[]{:S(2)}) async-start(f32[16,4,256]{2,1,0:T(4,128)} %get-tuple-element.33), calls=%async_computation.2 | async-start | bytes 131072 | tf_op jit(solution)/shard_map/all_to_all | solution.py:566
  49.2 4.5 %shard_map.126 = (f32[2,64,256]{2,1,0:T(8,128)S(1)}, f32[2,3,128,256]{3,2,1,0:T(8,128)S(1)}, f32[2,64,256]{2,1,0:T(8,128)S(1)}, f32[2,3,128,256]{3,2,1,0:T(8,128)S(1)}) custom-call(s32[1]{0:T(128)} %bitcast.4.me_ref, bf16[4,2,1024,256]{3,2,1,0:T(8,128)(2,1)} %get-tuple-element.34.slope_in, bf16[3,2,256,1024]{3,2,1,0:T(8,128)(2,1)} %get-tuple-element.35.actt_in, ...), custom_call_target="tpu_custom_call" | custom-call | flops 5000000000 | tf_op jit(solution)/shard_map/pallas_call | solution.py:441
  53.7 0.3 collective-permute-start.1
  54.0 0.2 collective-permute-start
  54.3 1.7 %all-to-all-done.2.heads_ref = f32[16,4,256]{2,1,0:T(4,128)S(1)} async-done(((f32[16,4,256]{2,1,0:T(4,128)}), f32[16,4,256]{2,1,0:T(4,128)S(1)}, u32[]{:S(2)}, u32[]{:S(2)}) %all-to-all-start.2) | async-done | bytes 65568 | tf_op jit(solution)/shard_map/all_to_all | solution.py:566
  56.0 0.2 collective-permute-done.refs_2_
  56.2 0.0 collective-permute-done.1.refs_3_
  56.2 1.0 %shard_map.127 = (f32[2,64,256]{2,1,0:T(8,128)}, f32[2,3,128,256]{3,2,1,0:T(8,128)}, f32[4,256]{1,0:T(4,128)}) custom-call(f32[4,256]{1,0:T(4,128)S(1)} %shard_map.125.head_ref, f32[2,64,256]{2,1,0:T(8,128)S(1)} %get-tuple-element.38.refs_0_, f32[2,3,128,256]{3,2,1,0:T(8,128)S(1)} %get-tuple-element.39.refs_1_, ...), custom_call_target="tpu_custom_call" | custom-call | tf_op jit(solution)/shard_map/pallas_call | solution.py:441
  (1 shorter events, 0.0 us)
Async XLA Ops:
  3.7 23.1 %all-to-all-start = ((bf16[8,288,128]{2,1,0:T(8,128)(2,1)}), bf16[8,288,128]{2,1,0:T(8,128)(2,1)S(1)}, u32[]{:S(2)}, u32[]{:S(2)}) async-start(bf16[8,288,128]{2,1,0:T(8,128)(2,1)} %shard_map.120), calls=%async_computation | async-start | bytes 1179648 | tf_op jit(solution)/shard_map/all_to_all | solution.py:503
  31.6 11.0 %all-to-all-start.1 = ((bf16[8,64,128]{2,1,0:T(8,128)(2,1)}), bf16[8,64,128]{2,1,0:T(8,128)(2,1)S(1)}, u32[]{:S(2)}, u32[]{:S(2)}) async-start(bf16[8,64,128]{2,1,0:T(8,128)(2,1)} %get-tuple-element.29), calls=%async_computation.1 | async-start | bytes 262144 | tf_op jit(solution)/shard_map/all_to_all | solution.py:525
  45.6 10.4 %all-to-all-start.2 = ((f32[16,4,256]{2,1,0:T(4,128)}), f32[16,4,256]{2,1,0:T(4,128)S(1)}, u32[]{:S(2)}, u32[]{:S(2)}) async-start(f32[16,4,256]{2,1,0:T(4,128)} %get-tuple-element.33), calls=%async_computation.2 | async-start | bytes 131072 | tf_op jit(solution)/shard_map/all_to_all | solution.py:566
  53.7 2.5 %collective-permute-start.1 = (f32[2,3,128,256]{3,2,1,0:T(8,128)S(1)}, f32[2,3,128,256]{3,2,1,0:T(8,128)S(1)}, u32[]{:S(2)}, u32[]{:S(2)}) collective-permute-start(f32[2,3,128,256]{3,2,1,0:T(8,128)S(1)} %get-tuple-element.41), channel_id=1, source_target_pairs={{0,1},{1,0},{2,3},{3,2},{4,5},{5,4},{6,7},{7,6},{8,9},{9,8},{10,11... | collective-permute-start | bytes 2359304 | tf_op jit(solution)/shard_map/ppermute | solution.py:592
  54.0 2.2 %collective-permute-start = (f32[2,64,256]{2,1,0:T(8,128)S(1)}, f32[2,64,256]{2,1,0:T(8,128)S(1)}, u32[]{:S(2)}, u32[]{:S(2)}) collective-permute-start(f32[2,64,256]{2,1,0:T(8,128)S(1)} %get-tuple-element.40), channel_id=1, source_target_pairs={{0,1},{1,0},{2,3},{3,2},{4,5},{5,4},{6,7},{7,6},{8,9},{9,8},{10,11... | collective-permute-start | bytes 393224 | tf_op jit(solution)/shard_map/ppermute | solution.py:592
